TPU v7x, 128 devices: a whole 4x4x4 slice. The times are simulated.
128 devices in a mesh: rep: 8 (over x, core), tp: 16 (over y, z).
Axes of the slice: x: 4, y: 4, z: 4, core: 2. Of those that a mesh axis runs over, the one named last changes fastest.
Arguments:
- queries: bfloat16 [4, 512, 8192], P(None, 'rep', 'tp'), may hold values from -128 to 128
- new_kv: bfloat16 [4, 512, 2048], P(None, 'rep'), may hold values from -4 to 4
- kv_cache: bfloat16 [256, 512, 4096], P('rep', None, 'tp'), may hold values from -12 to 12
- lengths: int32 [4, 512], P(None, 'rep'), may hold values from 1 to 512, as said below
- adapter_ids: int32 [4, 512], P(None, 'rep'), may hold values from 0 to 127, as said below
- owner_slot: int32 [128], replicated, may hold values from 0 to 127, as said below
- panels: bfloat16 [128, 8192, 128], P(('rep', 'tp')), may hold values from -0.1875 to 0.1875
- out_weight: bfloat16 [8192, 8192], P('tp'), may hold values from -0.0625 to 0.0625
Outputs:
- mixed: bfloat16 [4, 512, 8192], P(None, 'rep', 'tp')
Inputs may be any that keep to these rules, and one draw needn't show every extreme that they name: `lengths`: in each step some request has exactly 512 cached tokens. `adapter_ids`: pool slot s lies on the device of index s // 1 in rep+tp order. In each step, among the 64 requests of one replica (aligned blocks of 64 rows), at most 16 have adapters whose slots lie on any one replica, and exactly 16 on some replica. `owner_slot`: A permutation.
All inputs are finite; a program needn't handle non-finite values.
Results may differ from a plain program's by a relative error of at most 0.0095.
Values may be sent and summed in bfloat16 or wider, within the bound.
A program may use at most 256 MiB of HBM per device.

v0:
```python
import math

import jax
import jax.numpy as jnp
from jax import lax
from jax.sharding import PartitionSpec as P

KVH = 8
HD = 128
RANK = 64


ADAPTER_SCALING = 2.0
MASKED = -1e30


def from_partner(block, axis, bit):
    count = lax.axis_size(axis)
    route = []
    for low in range(count):
        high = low | 1 << bit
        if high != low and high < count:
            route += [(low, high), (high, low)]
    return lax.ppermute(block, axis, route)


def attend(group_queries, cache_rows, fresh_rows, lengths_mine, position_ids):
    head_size = group_queries.shape[-1]
    scale_factor = 1.0 / math.sqrt(head_size)
    cached_keys = cache_rows[:, :, :head_size]
    cached_values = cache_rows[:, :, head_size:]
    valid_mask = (position_ids[None, :] < lengths_mine[:, None])[:, None, :]
    scores = (
        jnp.einsum("nhd,npd->nhp", group_queries, cached_keys, preferred_element_type=jnp.float32)
        * scale_factor
    )
    scores = jnp.where(valid_mask, scores, MASKED)
    own_score = (
        jnp.einsum(
            "nhd,nd->nh",
            group_queries,
            fresh_rows[:, :head_size],
            preferred_element_type=jnp.float32,
        )
        * scale_factor
    )
    top_score = jnp.maximum(jnp.max(scores, axis=-1), own_score)
    weights = jnp.where(valid_mask, jnp.exp(scores - top_score[..., None]), 0.0)
    own_weight = jnp.exp(own_score - top_score)
    denominator = jnp.sum(weights, axis=-1) + own_weight
    mixed_values = jnp.einsum(
        "nhp,npd->nhd",
        weights.astype(jnp.bfloat16),
        cached_values,
        preferred_element_type=jnp.float32,
    )
    mixed_values = mixed_values + jnp.einsum(
        "nh,nd->nhd",
        own_weight.astype(jnp.bfloat16),
        fresh_rows[:, head_size:],
        preferred_element_type=jnp.float32,
    )
    return (mixed_values / denominator[..., None]).astype(jnp.bfloat16)


def shrink_terms(act_rows, row_sections):
    return jnp.einsum(
        "nw,nwk->nk", act_rows, row_sections[:, :, :RANK], preferred_element_type=jnp.float32
    )


def expand_products(shrink_project, row_sections):
    return jnp.einsum(
        "nk,nwk->nw", shrink_project, row_sections[:, :, RANK:], preferred_element_type=jnp.float32
    )


def shards(queries, new_kv, kv_cache, lengths, adapter_ids, owner_slot, panels, out_weight):
    tp_count = lax.axis_size("tp")
    rep_count = lax.axis_size("rep")
    tp_index = lax.axis_index("tp")
    group_size = tp_count // KVH
    member = tp_index % group_size
    kv_head = tp_index // group_size
    step_count, row_count, own_width = queries.shape
    half_rows = row_count // group_size
    pool_own = panels.shape[0]
    slice_width = out_weight.shape[0]
    position_ids = jnp.arange(kv_cache.shape[1], dtype=jnp.int32)
    fresh_all = lax.dynamic_slice_in_dim(new_kv, kv_head * 2 * HD, 2 * HD, 2)
    mine_start = member * half_rows
    other_start = (1 - member) * half_rows
    split_panels = panels.reshape(pool_own, tp_count, slice_width, 2 * RANK).transpose(1, 0, 2, 3)
    tiled_slices = jnp.broadcast_to(split_panels[None], (rep_count,) + split_panels.shape)
    tiled_slices = tiled_slices.reshape(rep_count * tp_count * pool_own, slice_width, 2 * RANK)
    adapter_slices = lax.all_to_all(
        tiled_slices, ("rep", "tp"), split_axis=0, concat_axis=0, tiled=True
    )
    adapter_range = jnp.arange(owner_slot.shape[0], dtype=jnp.int32)
    result_list = []
    for step_index in range(step_count):
        own_queries = queries[step_index]
        fresh_rows = lax.dynamic_slice_in_dim(fresh_all[step_index], mine_start, half_rows, 0)
        lengths_mine = lax.dynamic_slice_in_dim(lengths[step_index], mine_start, half_rows, 0)
        outgoing = lax.dynamic_slice_in_dim(own_queries, other_start, half_rows, 0)
        incoming = from_partner(outgoing, "tp", 0)
        own_part = lax.dynamic_slice_in_dim(own_queries, mine_start, half_rows, 0)
        group_queries = jnp.where(
            member == 0,
            jnp.concatenate([own_part, incoming], 1),
            jnp.concatenate([incoming, own_part], 1),
        )
        attended = attend(
            group_queries.reshape(half_rows, -1, HD),
            kv_cache,
            fresh_rows,
            lengths_mine,
            position_ids,
        )
        attended = attended.reshape(half_rows, -1)
        kept_heads = lax.dynamic_slice_in_dim(attended, member * own_width, own_width, 1)
        sending = lax.dynamic_slice_in_dim(attended, (1 - member) * own_width, own_width, 1)
        returned = from_partner(sending, "tp", 0)
        attn_rows = jnp.where(
            member == 0,
            jnp.concatenate([kept_heads, returned], 0),
            jnp.concatenate([returned, kept_heads], 0),
        )
        base_output = lax.psum_scatter(
            lax.dot_general(
                out_weight, attn_rows, (((0,), (1,)), ((), ())), preferred_element_type=jnp.float32
            ),
            "tp",
            scatter_dimension=0,
            tiled=True,
        ).T
        id_match = adapter_ids[step_index][:, None] == adapter_range[None, :]
        slot_now = jnp.sum(jnp.where(id_match, owner_slot[None, :], 0), axis=1)
        row_sections = adapter_slices[slot_now]
        shrink_part = shrink_terms(attn_rows, row_sections)
        shrink_project = lax.psum(shrink_part, "tp").astype(jnp.bfloat16)
        lowrank_update = expand_products(shrink_project, row_sections)
        result_list.append((base_output + ADAPTER_SCALING * lowrank_update).astype(jnp.bfloat16))
    return jnp.stack(result_list, 0)


def solution(mesh):
    placed = (
        P(None, "rep", "tp"),
        P(None, "rep", None),
        P("rep", None, "tp"),
        P(None, "rep"),
        P(None, "rep"),
        P(),
        P(("rep", "tp"), None, None),
        P("tp", None),
    )
    return jax.shard_map(
        shards, mesh=mesh, in_specs=placed, out_specs=P(None, "rep", "tp"), check_vma=False
    )
```

profile of v0, /device:TPU:0, one launch (start us, length us, event | category | flops | bytes accessed | tf_op | source)
XLA Modules:
  0.0 541.4 jit_solution(18154693473473498487)
XLA Ops:
  6.5 7.1 %broadcast_in_dim.117 = bf16[8,16,512,128]{3,2,1,0:T(8,128)(2,1)} broadcast(bf16[16,512,128]{2,1,0:T(8,128)(2,1)} %bitcast.179), dimensions={1,2,3} | broadcast | bytes 18874368 | tf_op jit(solution)/shard_map/broadcast_in_dim | solution.py:94
  13.6 11.7 %all-to-all-start = ((bf16[128,512,128]{2,1,0:T(8,128)(2,1)}), bf16[128,512,128]{2,1,0:T(8,128)(2,1)}, u32[]{:S(2)}, u32[]{:S(2)}) async-start(bf16[128,512,128]{2,1,0:T(8,128)(2,1)} %bitcast.178), calls=%async_computation.1 | async-start | bytes 33554432 | tf_op jit(solution)/shard_map/all_to_all | solution.py:96
  27.5 111.3 %collective-permute-done.6 = bf16[32,512]{1,0:T(8,128)(2,1)S(1)} collective-permute-done((bf16[32,512]{1,0:T(8,128)(2,1)S(1)}, bf16[32,512]{1,0:T(8,128)(2,1)S(1)}, u32[]{:S(2)}, u32[]{:S(2)}) %collective-permute-start.6) | collective-permute-done | bytes 32800 | tf_op jit(solution)/shard_map/ppermute | solution.py:24
  139.0 3.5 fusion.178
  145.8 4.6 collective-permute-done.7
  150.4 6.3 %convolution_bitcast_fusion = f32[8192,64]{0,1:T(8,128)} fusion(bf16[512,8192]{1,0:T(8,128)(2,1)} %param.15, bf16[32,512]{1,0:T(8,128)(2,1)S(1)} %collective-permute-done.7, bf16[32,512]{1,0:T(8,128)(2,1)S(1)} %get-tuple-element.34, pred[]{:T(512)S(6)} %eq.36), kind=kOutput, calls=%fused_computation.4 | convolution fusion | flops 537165824 | bytes 10551297 | tf_op jit(solution)/shard_map/dot_general | solution.py:130
  157.0 9.7 %collective-permute-done.4 = bf16[32,512]{1,0:T(8,128)(2,1)S(1)} collective-permute-done((bf16[32,512]{1,0:T(8,128)(2,1)S(1)}, bf16[32,512]{1,0:T(8,128)(2,1)S(1)}, u32[]{:S(2)}, u32[]{:S(2)}) %collective-permute-start.4) | collective-permute-done | bytes 32800 | tf_op jit(solution)/shard_map/ppermute | solution.py:24
  166.9 3.5 fusion.179
  173.7 13.1 %collective-permute-done.5 = bf16[32,512]{1,0:T(8,128)(2,1)S(1)} collective-permute-done((bf16[32,512]{1,0:T(8,128)(2,1)S(1)}, bf16[32,512]{1,0:T(8,128)(2,1)S(1)}, u32[]{:S(2)}, u32[]{:S(2)}) %collective-permute-start.5) | collective-permute-done | bytes 32800 | tf_op jit(solution)/shard_map/ppermute | solution.py:24
  186.8 6.3 %convolution_bitcast_fusion.1 = f32[8192,64]{0,1:T(8,128)} fusion(bf16[512,8192]{1,0:T(8,128)(2,1)} %param.15, bf16[32,512]{1,0:T(8,128)(2,1)S(1)} %collective-permute-done.5, bf16[32,512]{1,0:T(8,128)(2,1)S(1)} %get-tuple-element.30, pred[]{:T(512)S(6)} %eq.36), kind=kOutput, calls=%fused_computation.5 | convolution fusion | flops 537165824 | bytes 10551297 | tf_op jit(solution)/shard_map/dot_general | solution.py:130
  193.4 4.4 collective-permute-done.2
  198.0 3.5 fusion.180
  205.0 6.2 %collective-permute-done.3 = bf16[32,512]{1,0:T(8,128)(2,1)S(1)} collective-permute-done((bf16[32,512]{1,0:T(8,128)(2,1)S(1)}, bf16[32,512]{1,0:T(8,128)(2,1)S(1)}, u32[]{:S(2)}, u32[]{:S(2)}) %collective-permute-start.3) | collective-permute-done | bytes 32800 | tf_op jit(solution)/shard_map/ppermute | solution.py:24
  211.2 6.3 %convolution_bitcast_fusion.2 = f32[8192,64]{0,1:T(8,128)} fusion(bf16[512,8192]{1,0:T(8,128)(2,1)} %param.15, bf16[32,512]{1,0:T(8,128)(2,1)S(1)} %collective-permute-done.3, bf16[32,512]{1,0:T(8,128)(2,1)S(1)} %get-tuple-element.26, pred[]{:T(512)S(6)} %eq.36), kind=kOutput, calls=%fused_computation.6 | convolution fusion | flops 537165824 | bytes 10551297 | tf_op jit(solution)/shard_map/dot_general | solution.py:130
  222.3 3.5 fusion.181
  231.5 4.2 collective-permute-done.1
  235.7 6.3 %convolution_bitcast_fusion.3 = f32[8192,64]{0,1:T(8,128)} fusion(bf16[512,8192]{1,0:T(8,128)(2,1)} %param.15, bf16[32,512]{1,0:T(8,128)(2,1)S(1)} %collective-permute-done.1, bf16[32,512]{1,0:T(8,128)(2,1)S(1)} %get-tuple-element.22, pred[]{:T(512)S(6)} %eq.36), kind=kOutput, calls=%fused_computation.7 | convolution fusion | flops 537165824 | bytes 10551297 | tf_op jit(solution)/shard_map/dot_general | solution.py:130
  242.1 5.7 %all-to-all-done = bf16[128,512,128]{2,1,0:T(8,128)(2,1)} async-done(((bf16[128,512,128]{2,1,0:T(8,128)(2,1)}), bf16[128,512,128]{2,1,0:T(8,128)(2,1)}, u32[]{:S(2)}, u32[]{:S(2)}) %all-to-all-start) | async-done | bytes 16777248 | tf_op jit(solution)/shard_map/all_to_all | solution.py:96
  247.8 11.3 %gather_fusion.3 = bf16[64,512,128]{2,1,0:T(8,128)(2,1)} fusion(bf16[128,512,128]{2,1,0:T(8,128)(2,1)} %all-to-all-done, s32[1024]{0:T(1024)S(1)} %pad_clamp_fusion), kind=kCustom, calls=%fused_computation.3 | custom fusion | bytes 16777472 | tf_op jit(solution)/shard_map/gather | solution.py:139
  259.1 4.7 fusion.2
  263.8 11.5 %gather_fusion.2 = bf16[64,512,128]{2,1,0:T(8,128)(2,1)} fusion(bf16[128,512,128]{2,1,0:T(8,128)(2,1)} %all-to-all-done, s32[1024]{0:T(1024)S(1)} %pad_clamp_fusion.1), kind=kCustom, calls=%fused_computation.2 | custom fusion | bytes 16777472 | tf_op jit(solution)/shard_map/gather | solution.py:139
  275.3 4.6 fusion.6
  279.9 11.4 %gather_fusion.1 = bf16[64,512,128]{2,1,0:T(8,128)(2,1)} fusion(bf16[128,512,128]{2,1,0:T(8,128)(2,1)} %all-to-all-done, s32[1024]{0:T(1024)S(1)} %pad_clamp_fusion.2), kind=kCustom, calls=%fused_computation.1 | custom fusion | bytes 16777472 | tf_op jit(solution)/shard_map/gather | solution.py:139
  291.3 11.4 %gather_fusion = bf16[64,512,128]{2,1,0:T(8,128)(2,1)} fusion(bf16[128,512,128]{2,1,0:T(8,128)(2,1)} %all-to-all-done, s32[1024]{0:T(1024)S(1)} %pad_clamp_fusion.3), kind=kCustom, calls=%fused_computation | custom fusion | bytes 16777472 | tf_op jit(solution)/shard_map/gather | solution.py:139
  302.7 4.7 fusion.10
  309.6 102.5 %all-reduce = (bf16[64,64]{1,0:T(8,128)(2,1)S(1)}, bf16[64,64]{1,0:T(8,128)(2,1)S(1)}, bf16[64,64]{1,0:T(8,128)(2,1)S(1)}, bf16[64,64]{1,0:T(8,128)(2,1)S(1)}) all-reduce(f32[64,64]{1,0:T(8,128)S(1)} %bitcast.200, f32[64,64]{1,0:T(8,128)S(1)} %bitcast.201, f32[64,64]{1,0:T(8,128)S(1)} %bitcast.202, ...), channel_id=1, replica_groups=mesh['rep'=8,'tp'=16] {'tp'}, use_global_device_ids=true, to_apply=%region_19.20 | all-reduce | flops 16384 | bytes 98304 | tf_op jit(solution)/shard_map/psum | solution.py:141
  412.1 5.9 %fusion = f32[64,1,512]{2,1,0:T(1,128)S(1)} fusion(bf16[64,512,128]{2,1,0:T(8,128)(2,1)} %gather_fusion.3, bf16[64,64,1]{1,0,2:T(8,128)(2,1)S(1)} %bitcast.187), kind=kOutput, calls=%fused_computation.8 | convolution fusion | flops 4194304 | bytes 8527872 | tf_op jit(solution)/shard_map/nk,nwk->nw/dot_general | solution.py:73
  419.0 5.8 %fusion.4 = f32[64,1,512]{2,1,0:T(1,128)S(1)} fusion(bf16[64,512,128]{2,1,0:T(8,128)(2,1)} %gather_fusion.2, bf16[64,64,1]{1,0,2:T(8,128)(2,1)S(1)} %bitcast.186), kind=kOutput, calls=%fused_computation.12 | convolution fusion | flops 4194304 | bytes 8527872 | tf_op jit(solution)/shard_map/nk,nwk->nw/dot_general | solution.py:73
  425.7 5.8 %fusion.8 = f32[64,1,512]{2,1,0:T(1,128)S(1)} fusion(bf16[64,512,128]{2,1,0:T(8,128)(2,1)} %gather_fusion.1, bf16[64,64,1]{1,0,2:T(8,128)(2,1)S(1)} %bitcast.185), kind=kOutput, calls=%fused_computation.16 | convolution fusion | flops 4194304 | bytes 8527872 | tf_op jit(solution)/shard_map/nk,nwk->nw/dot_general | solution.py:73
  431.5 24.7 %reduce-scatter.7.cloned.1.call-done = f32[512,64]{0,1:T(8,128)} async-done(((f32[8192,64]{0,1:T(8,128)}), f32[512,64]{0,1:T(8,128)}) %reduce-scatter.7.cloned.1.call-update) | async-done | bytes 131088 | tf_op jit(solution)/shard_map/reduce_scatter | solution.py:129
  457.1 5.8 %fusion.12 = f32[64,1,512]{2,1,0:T(1,128)S(1)} fusion(bf16[64,512,128]{2,1,0:T(8,128)(2,1)} %gather_fusion, bf16[64,64,1]{1,0,2:T(8,128)(2,1)S(1)} %bitcast.184), kind=kOutput, calls=%fused_computation.20 | convolution fusion | flops 4194304 | bytes 8527872 | tf_op jit(solution)/shard_map/nk,nwk->nw/dot_general | solution.py:73
  462.8 70.4 %reduce-scatter.5.cloned.1.call-done = f32[512,64]{0,1:T(8,128)} async-done(((f32[8192,64]{0,1:T(8,128)}), f32[512,64]{0,1:T(8,128)}) %reduce-scatter.5.cloned.1.call-update) | async-done | bytes 131088 | tf_op jit(solution)/shard_map/reduce_scatter | solution.py:129
  (100 shorter events, 30.6 us)
Async XLA Ops:
  13.6 11.8 %copy-start.1 = (bf16[4,64,512]{2,1,0:T(8,128)(2,1)S(1)}, bf16[4,64,512]{2,1,0:T(8,128)(2,1)}, u32[]{:S(2)}) copy-start(bf16[4,64,512]{2,1,0:T(8,128)(2,1)} %param.8) | copy-start | bytes 786436
  13.6 12.9 %copy-start.2 = (s32[4,64]{1,0:T(4,128)S(1)}, s32[4,64]{1,0:T(4,128)}, u32[]{:S(2)}) copy-start(s32[4,64]{1,0:T(4,128)} %param.11) | copy-start | bytes 3076
  13.6 234.2 %all-to-all-start = ((bf16[128,512,128]{2,1,0:T(8,128)(2,1)}), bf16[128,512,128]{2,1,0:T(8,128)(2,1)}, u32[]{:S(2)}, u32[]{:S(2)}) async-start(bf16[128,512,128]{2,1,0:T(8,128)(2,1)} %bitcast.178), calls=%async_computation.1 | async-start | bytes 33554432 | tf_op jit(solution)/shard_map/all_to_all | solution.py:96
  25.3 392.7 %reduce-scatter.11.cloned.1.call-start = ((), (), s32[]{:S(2)}) async-start(), calls=%async_computation.8 | async-start | bytes 2228224 | tf_op jit(solution)/shard_map/reduce_scatter | solution.py:129
  25.4 113.4 %collective-permute-start.6 = (bf16[32,512]{1,0:T(8,128)(2,1)S(1)}, bf16[32,512]{1,0:T(8,128)(2,1)S(1)}, u32[]{:S(2)}, u32[]{:S(2)}) collective-permute-start(bf16[32,512]{1,0:T(8,128)(2,1)S(1)} %get-tuple-element.36), channel_id=1, source_target_pairs={{0,1},{1,0},{2,3},{3,2},{4,5},{5,4},{6,7},{7,6},{8,9},{9,8},{10,11... | collective-permute-start | bytes 98312 | tf_op jit(solution)/shard_map/ppermute | solution.py:24
  145.7 4.7 collective-permute-start.7
  156.7 268.0 %reduce-scatter.9.cloned.1.call-start = ((), (), s32[]{:S(2)}) async-start(), calls=%async_computation.7 | async-start | bytes 2228224 | tf_op jit(solution)/shard_map/reduce_scatter | solution.py:129
  156.8 9.9 %collective-permute-start.4 = (bf16[32,512]{1,0:T(8,128)(2,1)S(1)}, bf16[32,512]{1,0:T(8,128)(2,1)S(1)}, u32[]{:S(2)}, u32[]{:S(2)}) collective-permute-start(bf16[32,512]{1,0:T(8,128)(2,1)S(1)} %get-tuple-element.32), channel_id=1, source_target_pairs={{0,1},{1,0},{2,3},{3,2},{4,5},{5,4},{6,7},{7,6},{8,9},{9,8},{10,11... | collective-permute-start | bytes 98312 | tf_op jit(solution)/shard_map/ppermute | solution.py:24
  173.6 13.1 %collective-permute-start.5 = (bf16[32,512]{1,0:T(8,128)(2,1)S(1)}, bf16[32,512]{1,0:T(8,128)(2,1)S(1)}, u32[]{:S(2)}, u32[]{:S(2)}) collective-permute-start(bf16[32,512]{1,0:T(8,128)(2,1)S(1)} %get-tuple-element.29), channel_id=1, source_target_pairs={{0,1},{1,0},{2,3},{3,2},{4,5},{5,4},{6,7},{7,6},{8,9},{9,8},{10,11... | collective-permute-start | bytes 98312 | tf_op jit(solution)/shard_map/ppermute | solution.py:24
  193.0 263.1 %reduce-scatter.7.cloned.1.call-start = ((), (), s32[]{:S(2)}) async-start(), calls=%async_computation.6 | async-start | bytes 2228224 | tf_op jit(solution)/shard_map/reduce_scatter | solution.py:129
  193.1 4.7 collective-permute-start.2
  204.8 6.5 %collective-permute-start.3 = (bf16[32,512]{1,0:T(8,128)(2,1)S(1)}, bf16[32,512]{1,0:T(8,128)(2,1)S(1)}, u32[]{:S(2)}, u32[]{:S(2)}) collective-permute-start(bf16[32,512]{1,0:T(8,128)(2,1)S(1)} %get-tuple-element.25), channel_id=1, source_target_pairs={{0,1},{1,0},{2,3},{3,2},{4,5},{5,4},{6,7},{7,6},{8,9},{9,8},{10,11... | collective-permute-start | bytes 98312 | tf_op jit(solution)/shard_map/ppermute | solution.py:24
  211.2 9.0 %copy-start.3 = (s32[4,64]{1,0:T(4,128)S(1)}, s32[4,64]{1,0:T(4,128)}, u32[]{:S(2)}) copy-start(s32[4,64]{1,0:T(4,128)} %param.12) | copy-start | bytes 3076
  211.2 9.0 %copy-start.4 = (s32[128]{0:T(128)S(1)}, s32[128]{0:T(128)}, u32[]{:S(2)}) copy-start(s32[128]{0:T(128)} %param.13) | copy-start | bytes 1540
  217.6 315.6 %reduce-scatter.5.cloned.1.call-start = ((), (), s32[]{:S(2)}) async-start(), calls=%async_computation.5 | async-start | bytes 2228224 | tf_op jit(solution)/shard_map/reduce_scatter | solution.py:129
  217.7 4.4 collective-permute-start
  229.0 6.6 %collective-permute-start.1 = (bf16[32,512]{1,0:T(8,128)(2,1)S(1)}, bf16[32,512]{1,0:T(8,128)(2,1)S(1)}, u32[]{:S(2)}, u32[]{:S(2)}) collective-permute-start(bf16[32,512]{1,0:T(8,128)(2,1)S(1)} %get-tuple-element.21), channel_id=1, source_target_pairs={{0,1},{1,0},{2,3},{3,2},{4,5},{5,4},{6,7},{7,6},{8,9},{9,8},{10,11... | collective-permute-start | bytes 98312 | tf_op jit(solution)/shard_map/ppermute | solution.py:24
  302.7 5.8 %copy-start = (bf16[64,512,128]{2,1,0:T(8,128)(2,1)S(1)}, bf16[64,512,128]{2,1,0:T(8,128)(2,1)}, u32[]{:S(2)}) copy-start(bf16[64,512,128]{2,1,0:T(8,128)(2,1)} %gather_fusion) | copy-start | bytes 25165828
Sparse Core Ops, SparseCore 0:
  156.8 145.0 reduce-scatter.10
  305.6 73.6 reduce-scatter.8
  382.5 73.5 reduce-scatter.6
  459.6 73.5 reduce-scatter.4
where the time goes:
time: 543 us; the launch traced here: 541 us
  waiting for transfers between devices  256 us (47%)
  blocking collectives  102 us (19%)
  matrix products  89.7 us (17%)
  local copies, waits for them, and re-layouts  55 us (10%)
  starting transfers between devices  18.5 us (3%)
  between operations  13.6 us (3%)
  other arithmetic  6.32 us (1%)
    ppermute x8, waiting for transfers between devices, from_partner(): return lax.ppermute(block, axis, route)  155 us
    psum x1, blocking collectives, shards(): shrink_project = lax.psum(shrink_part, 'tp').astype(jnp.bfloat16)  102 us
    reduce_scatter x4, waiting for transfers between devices, shards(): lax.psum_scatter(lax.dot_general(out_weight, attn_rows, (((0,), (1,)), ((...  95.1 us
    gather x4, local copies, waits for them, and re-layouts, shards(): row_sections = adapter_slices[slot_now]  45.6 us
    dot_general x4, matrix products, shards(): lax.dot_general(out_weight, attn_rows, (((0,), (1,)), ((), ())), preferre...  25.2 us
    dot_general x4, matrix products, expand_products(): jnp.einsum('nk,nwk->nw', shrink_project, row_sections[:, :, RANK:], prefe...  23.2 us
    dot_general x4, matrix products, shrink_terms(): jnp.einsum('nw,nwk->nk', act_rows, row_sections[:, :, :RANK], preferred_e...  15.2 us
    dot_general x4, matrix products, attend(): jnp.einsum('nhd,npd->nhp', group_queries, cached_keys, preferred_element_...  13.8 us
  transfers between devices with their start and end apart: 13, of which 11 were waited for; matrix products, arithmetic and copies ran while one was open for 26% of the time, Pallas kernels for 0%

commit v1 on v0

v1 whole, which is shorter than its diff:
```python
import functools
import math

import jax
import jax.numpy as jnp
from jax import lax
from jax.experimental import pallas as pl
from jax.experimental.pallas import tpu as pltpu
from jax.sharding import PartitionSpec as P

MESH = pl.DeviceIdType.MESH
F32 = jnp.float32
BF16 = jnp.bfloat16

HD = 128
RANK = 64
CAP = 16
LANES = 128
KV_CHUNK = 4
ADAPTER_SCALING = 2.0
MASKED = -1e30


def nt_dot(a, b):
    return lax.dot_general(a, b, (((1,), (1,)), ((), ())), preferred_element_type=F32)


def tn_dot(a, b):
    return lax.dot_general(a, b, (((0,), (0,)), ((), ())), preferred_element_type=F32)


def dot(a, b):
    return jnp.dot(a, b, preferred_element_type=F32)


def iota(shape, dim):
    return lax.broadcasted_iota(jnp.int32, shape, dim)


def kernel(
    n_rep, n_tp, side,
    queries, new_kv, kv_cache, lengths, ids, owners, panels, weight,
    out,
    q_own, q_in, q_rows, o_rows, fresh, cache, w_buf, pan, spread, attn, attn_back, tags, place,
    send_y, recv_y, own_y, send_z, recv_z, own_z, fwd_a, got_a, fwd_b, got_b, base,
    disp, work, part, part_in, shrink, delta, delta_in,
    cache_sem, load_sem, q_sem, pan_send, pan_recv, back_sem,
    y_send, y_recv, z_send, z_recv, a_send, a_recv, b_send, b_recv,
    disp_send, disp_recv, part_send, part_recv, shr_send, shr_recv, del_send, del_recv,
):
    steps, rows, width = out.shape
    half = rows // 2
    heads = width // HD
    per_request = 2 * heads * steps
    total_rows = steps * rows
    part_width = width // 2
    bits = n_tp.bit_length() - 1
    cap_bits = CAP.bit_length() - 1

    rep = lax.axis_index("rep")
    t = lax.axis_index("tp")
    y, z = lax.div(t, side), lax.rem(t, side)
    member, group = lax.rem(t, 2), lax.div(t, 2)
    partner = t + 1 - 2 * member
    mine = pl.multiple_of(member * half, half)
    other = pl.multiple_of((1 - member) * half, half)

    def tp_peer(k):
        dy, dz = lax.div(k, side), lax.rem(k, side)
        return lax.rem(y + dy, side) * side + lax.rem(z + dz, side)

    def rep_peer(k):
        return lax.rem(rep + k, n_rep)

    def remote(src, dst, send, recv, device):
        return pltpu.make_async_remote_copy(
            src_ref=src, dst_ref=dst, send_sem=send, recv_sem=recv, device_id=device, device_id_type=MESH
        )

    def over(low, high, body):
        def run(k, carry):
            body(k)
            return carry

        lax.fori_loop(low, high, run, 0)

    load_q = pltpu.make_async_copy(queries.at[:, pl.ds(mine, half), :], q_own, load_sem.at[0])
    load_fresh = pltpu.make_async_copy(
        new_kv.at[:, pl.ds(mine, half), pl.ds(pl.multiple_of(group * 2 * HD, 2 * HD), 2 * HD)], fresh, load_sem.at[1]
    )
    load_w = pltpu.make_async_copy(weight, w_buf, load_sem.at[2])

    def load_cache(c):
        span = pl.ds(c * KV_CHUNK, KV_CHUNK)
        return pltpu.make_async_copy(kv_cache.at[span], cache.at[span], cache_sem.at[c])

    load_q.start()
    load_fresh.start()
    over(0, half // KV_CHUNK, lambda c: load_cache(c).start())
    load_w.start()

    barrier = pltpu.get_barrier_semaphore()
    over(1, n_tp, lambda k: pl.semaphore_signal(barrier, inc=1, device_id=(rep, tp_peer(k)), device_id_type=MESH))
    over(1, n_rep, lambda k: pl.semaphore_signal(barrier, inc=1, device_id=(rep_peer(k), t), device_id_type=MESH))
    pl.semaphore_wait(barrier, n_tp + n_rep - 2)

    swap_q = remote(queries.at[:, pl.ds(other, half), :], q_in, q_sem.at[0], q_sem.at[1], (rep, partner))
    swap_q.start()
    pan_cols = pl.ds(pl.multiple_of(t * LANES, LANES), LANES)

    def send_pan(k):
        peer = tp_peer(k)
        src = panels.at[0, pl.ds(pl.multiple_of(peer * width, width), width), :]
        return remote(src, pan.at[:, pan_cols], pan_send.at[k], pan_recv.at[k], (rep, peer))

    over(1, n_tp, lambda k: send_pan(k).start())
    keep_pan = pltpu.make_async_copy(
        panels.at[0, pl.ds(pl.multiple_of(t * width, width), width), :], pan.at[:, pan_cols], load_sem.at[3]
    )
    keep_pan.start()

    n_dest = n_rep * CAP
    n_adapters = owners.shape[1]
    diagonal = iota((rows, rows), 0) == iota((rows, rows), 1)
    earlier = jnp.where(iota((rows, rows), 1) < iota((rows, rows), 0), 1.0, 0.0).astype(BF16)
    dest = iota((rows, n_dest), 1)
    for s in range(steps):
        id_row = jnp.broadcast_to(ids[s : s + 1, :].astype(F32), (rows, rows))
        id_col = jnp.sum(jnp.where(diagonal, id_row, 0.0), axis=1, keepdims=True)
        found = iota((rows, n_adapters), 1).astype(F32) == id_col
        owner_row = jnp.broadcast_to(owners[...].astype(F32), (rows, n_adapters))
        slot = jnp.sum(jnp.where(found, owner_row, 0.0), axis=1, keepdims=True).astype(jnp.int32)
        holder = lax.shift_right_logical(slot, bits)
        goes = lax.shift_right_logical(dest, cap_bits) == holder
        rank = dot(earlier, jnp.where(goes, 1.0, 0.0).astype(BF16))
        here = goes & (rank == (dest & (CAP - 1)).astype(F32))
        place[s] = jnp.where(here, 1.0, 0.0).astype(BF16)
        tags[s] = jnp.where(iota((rows, LANES), 1) == (slot & (n_tp - 1)), 1.0, 0.0).astype(BF16)
    spread[...] = jnp.where(
        iota(spread.shape, 0) == lax.shift_right_logical(iota(spread.shape, 1), 7), 1.0, 0.0
    ).astype(BF16)

    load_q.wait()
    load_fresh.wait()
    swap_q.wait()
    for s in range(steps):
        for h in range(heads):
            cols = slice(h * HD, (h + 1) * HD)
            q_rows[pl.ds(h * steps + s, half, stride=per_request), :] = q_own[s, :, cols].astype(F32)
            q_rows[pl.ds((heads + h) * steps + s, half, stride=per_request), :] = q_in[s, :, cols].astype(F32)

    scale = 1.0 / math.sqrt(HD)
    positions = cache.shape[1]

    def attend(i):
        q = q_rows[pl.ds(pl.multiple_of(i * per_request, per_request), per_request), :].astype(BF16)
        step_of = iota((per_request, 1), 0) & (steps - 1)
        limit = jnp.zeros((per_request, 1), jnp.int32)
        for s in range(steps):
            limit = jnp.where(step_of == s, lengths[s, mine + i], limit)
        fresh_rows = fresh[...].reshape(steps * half, 2 * HD)
        scores = nt_dot(q, cache[i, :, :HD]) * scale
        scores = jnp.where(iota(scores.shape, 1) < limit, scores, MASKED)
        own = nt_dot(q, fresh_rows[:, :HD]) * scale
        own = jnp.where(iota(own.shape, 1) == step_of * half + i, own, MASKED)
        top = jnp.maximum(jnp.max(scores, axis=1, keepdims=True), jnp.max(own, axis=1, keepdims=True))
        scores = jnp.exp(scores - top)
        own = jnp.exp(own - top)
        total = jnp.sum(scores, axis=1, keepdims=True) + jnp.sum(own, axis=1, keepdims=True)
        mixed = dot(scores.astype(BF16), cache[i, :, HD:]) + dot(own.astype(BF16), fresh_rows[:, HD:])
        o_rows[pl.ds(pl.multiple_of(i * per_request, per_request), per_request), :] = mixed / total

    def attend_chunk(c):
        load_cache(c).wait()
        for j in range(KV_CHUNK):
            attend(c * KV_CHUNK + j)

    over(0, half // KV_CHUNK, attend_chunk)

    for s in range(steps):
        for h in range(heads):
            cols = slice(h * HD, (h + 1) * HD)
            own_heads = o_rows[pl.ds(h * steps + s, half, stride=per_request), :]
            attn[s, pl.ds(mine, half), cols] = own_heads.astype(BF16)
            far_heads = o_rows[pl.ds((heads + h) * steps + s, half, stride=per_request), :]
            attn_back[s, :, cols] = far_heads.astype(BF16)
    swap_back = remote(
        attn_back, attn.at[:, pl.ds(mine, half), :], back_sem.at[0], back_sem.at[1], (rep, partner)
    )
    swap_back.start()
    swap_back.wait()

    for s in range(steps):
        span = slice(s * CAP, (s + 1) * CAP)
        routed = tn_dot(place[s], attn[s]).astype(BF16)
        disp[:, span, :width] = routed.reshape(n_rep, CAP, width)
        disp[:, span, width:] = tn_dot(place[s], tags[s]).astype(BF16).reshape(n_rep, CAP, LANES)

    def send_disp(k):
        peer = rep_peer(k)
        return remote(disp.at[peer], work.at[rep], disp_send.at[k], disp_recv.at[k], (peer, t))

    over(1, n_rep, lambda k: send_disp(k).start())
    work[rep] = disp[rep]

    load_w.wait()

    def project(block, part):
        cols = pl.ds(pl.multiple_of(block * width + part * part_width, part_width), part_width)
        return dot(attn[...].reshape(total_rows, width), w_buf[:, cols])

    def along_y(d, j):
        device = (rep, lax.rem(y + d, side) * side + z)
        return remote(send_y.at[d - 1, j], recv_y.at[d - 1, j], y_send.at[d - 1, j], y_recv.at[d - 1, j], device)

    def along_z(d, j):
        device = (rep, y * side + lax.rem(z + d, side))
        return remote(send_z.at[d - 1, j], recv_z.at[d - 1, j], z_send.at[d - 1, j], z_recv.at[d - 1, j], device)

    def first_stage(j):
        to_z = lax.rem(z + 1 + j, side)
        to_y = lax.rem(y + 1 + j, side)
        for d in range(1, side):
            send_y[d - 1, j] = project(lax.rem(y + d, side) * side + to_z, 0).astype(BF16)
            along_y(d, j).start()
            send_z[d - 1, j] = project(to_y * side + lax.rem(z + d, side), 1).astype(BF16)
            along_z(d, j).start()
        own_y[j] = project(y * side + to_z, 0)
        own_z[j] = project(to_y * side + z, 1)

    over(0, side, first_stage)

    keep_pan.wait()
    over(1, n_tp, lambda k: send_pan(k).wait_recv())
    over(1, n_rep, lambda k: send_disp(k).wait_recv())
    work_rows = n_rep * steps * CAP
    packed_rows = work_rows // 2
    tile = min(128, packed_rows)
    tile_reps = tile // (steps * CAP)
    low_lanes = iota((tile, LANES), 1) < RANK

    def masks(tags_rows):
        return dot(tags_rows, spread[...])

    def shrink_tile(c):
        x = work[pl.ds(c * tile_reps, tile_reps)].reshape(tile, width + LANES)
        products = dot(x[:, :width], pan[...]) * masks(x[:, width:])
        total = products[:, :LANES]
        for a in range(1, n_tp):
            total = total + products[:, a * LANES : (a + 1) * LANES]
        return total

    n_tiles = packed_rows // tile

    def shrink_pair(c):
        first = shrink_tile(c)
        second = pltpu.roll(shrink_tile(n_tiles + c), RANK, 1)
        part[pl.ds(pl.multiple_of(c * tile, tile), tile), :] = jnp.where(low_lanes, first, second)

    over(0, n_tiles, shrink_pair)

    slab = packed_rows // n_tp

    def slab_of(device):
        return pl.ds(pl.multiple_of(device * slab, slab), slab)

    def send_part(k):
        peer = tp_peer(k)
        return remote(part.at[slab_of(peer)], part_in.at[k], part_send.at[k], part_recv.at[k], (rep, peer))

    over(1, n_tp, lambda k: send_part(k).start())

    def forward_y(j):
        device = (rep, y * side + lax.rem(z + 1 + j, side))
        return remote(fwd_a.at[j], got_a.at[j], a_send.at[j], a_recv.at[j], device)

    def forward_z(j):
        device = (rep, lax.rem(y + 1 + j, side) * side + z)
        return remote(fwd_b.at[j], got_b.at[j], b_send.at[j], b_recv.at[j], device)

    def gathered(own, recv, copy, j):
        total = own[j]
        for d in range(1, side):
            copy(d, j).wait_recv()
            total = total + recv[d - 1, j].astype(F32)
        return total

    def second_stage(j):
        fwd_a[j] = gathered(own_y, recv_y, along_y, j).astype(BF16)
        forward_y(j).start()
        fwd_b[j] = gathered(own_z, recv_z, along_z, j).astype(BF16)
        forward_z(j).start()

    second_stage(0)

    over(1, n_tp, lambda k: send_part(k).wait_recv())
    total = part[slab_of(t), :]
    for k in range(1, n_tp):
        total = total + part_in[k]
    shrink[slab_of(t), :] = total.astype(BF16)

    def send_shrink(k):
        peer = tp_peer(k)
        return remote(shrink.at[slab_of(t)], shrink.at[slab_of(t)], shr_send.at[k], shr_recv.at[k], (rep, peer))

    over(1, n_tp, lambda k: send_shrink(k).start())
    over(1, side - 1, second_stage)

    over(1, n_tp, lambda k: send_shrink(k).wait_recv())

    def expand_tile(c, low):
        shrunk = shrink[pl.ds(pl.multiple_of(c * tile, tile), tile), :].astype(F32)
        if low:
            shrunk = pltpu.roll(shrunk, RANK, 1)
        shrunk = jnp.where(low_lanes, 0.0, shrunk)
        at = c if low else n_tiles + c
        tag = work[pl.ds(at * tile_reps, tile_reps), :, width:].reshape(tile, LANES)
        picked = (masks(tag) * jnp.concatenate([shrunk] * n_tp, axis=1)).astype(BF16)
        result = nt_dot(picked, pan[...]).astype(BF16)
        delta[pl.ds(at * tile_reps, tile_reps)] = result.reshape(tile_reps, steps * CAP, width)

    def expand_pair(c):
        expand_tile(c, True)
        expand_tile(c, False)

    over(0, n_tiles, expand_pair)

    def send_delta(k):
        peer = rep_peer(k)
        return remote(delta.at[peer], delta_in.at[rep], del_send.at[k], del_recv.at[k], (peer, t))

    over(1, n_rep, lambda k: send_delta(k).start())
    delta_in[rep] = delta[rep]

    last = side - 1
    base[:, :part_width] = gathered(own_y, recv_y, along_y, last)
    base[:, part_width:] = gathered(own_z, recv_z, along_z, last)
    for j in range(last):
        forward_y(j).wait_recv()
        base[:, :part_width] += got_a[j].astype(F32)
        forward_z(j).wait_recv()
        base[:, part_width:] += got_b[j].astype(F32)

    over(1, n_rep, lambda k: send_delta(k).wait_recv())
    for s in range(steps):
        rows_in = delta_in[:, s * CAP : (s + 1) * CAP, :].reshape(n_dest, width)
        update = dot(place[s], rows_in)
        out[s] = (base[s * rows : (s + 1) * rows, :] + ADAPTER_SCALING * update).astype(BF16)

    def drain_tp(k):
        send_pan(k).wait_send()
        send_part(k).wait_send()
        send_shrink(k).wait_send()

    def drain_rep(k):
        send_disp(k).wait_send()
        send_delta(k).wait_send()

    def drain_sums(j):
        for d in range(1, side):
            along_y(d, j).wait_send()
            along_z(d, j).wait_send()

    def drain_forward(j):
        forward_y(j).wait_send()
        forward_z(j).wait_send()

    over(1, n_tp, drain_tp)
    over(1, n_rep, drain_rep)
    over(0, side, drain_sums)
    over(0, side - 1, drain_forward)


def shards(n_rep, n_tp, queries, new_kv, kv_cache, lengths, adapter_ids, owner_slot, panels, out_weight):
    side = math.isqrt(n_tp)
    steps, rows, width = queries.shape
    half = rows // 2
    heads = width // HD
    total = steps * rows
    part = width // 2
    per_request = 2 * heads * steps
    work_rows = n_rep * steps * CAP
    dma = pltpu.SemaphoreType.DMA
    vmem = pltpu.VMEM
    hop = side - 1
    scratch = [
        vmem((steps, half, width), BF16),
        vmem((steps, half, width), BF16),
        vmem((half * per_request, HD), F32),
        vmem((half * per_request, HD), F32),
        vmem((steps, half, 2 * HD), BF16),
        vmem(kv_cache.shape, BF16),
        vmem(out_weight.shape, BF16),
        vmem((width, n_tp * LANES), BF16),
        vmem((LANES, n_tp * LANES), BF16),
        vmem((steps, rows, width), BF16),
        vmem((steps, half, width), BF16),
        vmem((steps, rows, LANES), BF16),
        vmem((steps, rows, n_rep * CAP), BF16),
        vmem((hop, side, total, part), BF16),
        vmem((hop, side, total, part), BF16),
        vmem((side, total, part), F32),
        vmem((hop, side, total, part), BF16),
        vmem((hop, side, total, part), BF16),
        vmem((side, total, part), F32),
        vmem((hop, total, part), BF16),
        vmem((hop, total, part), BF16),
        vmem((hop, total, part), BF16),
        vmem((hop, total, part), BF16),
        vmem((total, width), F32),
        vmem((n_rep, steps * CAP, width + LANES), BF16),
        vmem((n_rep, steps * CAP, width + LANES), BF16),
        vmem((work_rows // 2, LANES), F32),
        vmem((n_tp, work_rows // 2 // n_tp, LANES), F32),
        vmem((work_rows // 2, LANES), BF16),
        vmem((n_rep, steps * CAP, width), BF16),
        vmem((n_rep, steps * CAP, width), BF16),
        dma((half // KV_CHUNK,)),
        dma((4,)),
        dma((2,)),
        dma((n_tp,)), dma((n_tp,)),
        dma((2,)),
        dma((hop, side)), dma((hop, side)),
        dma((hop, side)), dma((hop, side)),
        dma((hop,)), dma((hop,)),
        dma((hop,)), dma((hop,)),
        dma((n_rep,)), dma((n_rep,)),
        dma((n_tp,)), dma((n_tp,)),
        dma((n_tp,)), dma((n_tp,)),
        dma((n_rep,)), dma((n_rep,)),
    ]
    hbm = pl.BlockSpec(memory_space=pl.ANY)
    in_vmem = pl.BlockSpec(memory_space=pltpu.VMEM)
    in_smem = pl.BlockSpec(memory_space=pltpu.SMEM)
    return pl.pallas_call(
        functools.partial(kernel, n_rep, n_tp, side),
        out_shape=jax.ShapeDtypeStruct(queries.shape, BF16),
        in_specs=[hbm, hbm, hbm, in_smem, in_vmem, in_vmem, hbm, hbm],
        out_specs=in_vmem,
        scratch_shapes=scratch,
        compiler_params=pltpu.CompilerParams(
            collective_id=0, has_side_effects=True, vmem_limit_bytes=56 * 1024 * 1024
        ),
        cost_estimate=pl.CostEstimate(
            flops=5_000_000_000, bytes_accessed=20_000_000, transcendentals=600_000
        ),
    )(queries, new_kv, kv_cache, lengths, adapter_ids, owner_slot.reshape(1, -1), panels, out_weight)


def solution(mesh):
    placed = (
        P(None, "rep", "tp"),
        P(None, "rep", None),
        P("rep", None, "tp"),
        P(None, "rep"),
        P(None, "rep"),
        P(),
        P(("rep", "tp"), None, None),
        P("tp", None),
    )
    return jax.shard_map(
        functools.partial(shards, mesh.shape["rep"], mesh.shape["tp"]),
        mesh=mesh, in_specs=placed, out_specs=P(None, "rep", "tp"), check_vma=False,
    )
```

time: 543 us -> 88.9 us (0.16)
  waiting for transfers between devices: 256 us -> 0 us
  blocking collectives: 102 us -> 0 us
  matrix products: 89.7 us -> 0 us
  Pallas kernels: 0 us -> 85.7 us
  local copies, waits for them, and re-layouts: 55 us -> 1.67 us
  starting transfers between devices: 18.5 us -> 0 us
  between operations: 13.6 us -> 0.01 us
  other arithmetic: 6.32 us -> 0 us
    ppermute x8 -> x0, waiting for transfers between devices: 155 us -> none  [from_partner(): return lax.ppermute(block, axis, route)]
    psum x1 -> x0, blocking collectives: 102 us -> none  [shards(): shrink_project = lax.psum(shrink_part, 'tp').astype(jnp.bfloat16)]
    reduce_scatter x4 -> x0, waiting for transfers between devices: 95.1 us -> none  [shards(): lax.psum_scatter(lax.dot_general(out_weight, attn_rows, (((0,), (1,)), ((...]
    dot_general x24 -> x0, matrix products: 89.7 us -> none  [the longest x4 25.2 us: shards(): lax.dot_general(out_weight, attn_rows, (((0,), (1,)), ((), ())), preferre...]
    pallas_call x0 -> x1, Pallas kernels: none -> 85.7 us  [shards(): pl.pallas_call(functools.partial(kernel, n_rep, n_tp, side), out_shape=ja...]
    gather x4 -> x0, local copies, waits for them, and re-layouts: 45.6 us -> none  [shards(): row_sections = adapter_slices[slot_now]]
    all_to_all x1 -> x0, starting transfers between devices: 11.7 us -> none  [shards(): lax.all_to_all(tiled_slices, ('rep', 'tp'), split_axis=0, concat_axis=0,...]
    broadcast_in_dim x1 -> x0, local copies, waits for them, and re-layouts: 7.06 us -> none  [shards(): jnp.broadcast_to(split_panels[None], (rep_count,) + split_panels.shape)]
  transfers between devices with their start and end apart: 13 -> 0, of which waited for: 11 -> 0; matrix products, arithmetic and copies ran while one was open for 26% -> 0% of each run, Pallas kernels for 0% -> 0%
where the time goes in v1:
time: 88.9 us; the launch traced here: 87.3 us
  Pallas kernels  85.7 us (96%)
  local copies, waits for them, and re-layouts  1.67 us (2%)
    pallas_call x1, Pallas kernels, shards(): pl.pallas_call(functools.partial(kernel, n_rep, n_tp, side), out_shape=ja...  85.7 us

profile of v1, /device:TPU:0, one launch (start us, length us, event | category | flops | bytes accessed | tf_op | source)
XLA Modules:
  0.0 87.3 jit_solution(11349239879393986662)
XLA Ops:
  0.0 85.7 %shard_map.82 = bf16[4,64,512]{2,1,0:T(8,128)(2,1)} custom-call(bf16[4,64,512]{2,1,0:T(8,128)(2,1)} %queries.1, bf16[4,64,2048]{2,1,0:T(8,128)(2,1)} %new_kv.1, bf16[32,512,256]{2,1,0:T(8,128)(2,1)} %kv_cache.1, s32[4,64]{1,0:T(4,128)} %lengths.1, s32[4,64]{1,0:T(4,128)} %ids.1, s32[1,128]{1,0:T(1,128)} %bitcast.1, bf16[1,8192,128]{2,1,0:T(8,128)(2,1)} %panels.1, ...), custom_call_target="tpu_custom_call" | custom-call | flops 5000000000 | bytes 20000000 | tf_op jit(solution)/shard_map/pallas_call | solution.py:435
  85.7 1.7 %copy.10 = bf16[4,64,512]{2,1,0:T(8,128)(2,1)} copy(bf16[4,64,512]{2,1,0:T(8,128)(2,1)} %shard_map.82) | data formatting | bytes 524288

commit v2 on v1

v2 whole, which is shorter than its diff:
```python
import functools
import math

import jax
import jax.numpy as jnp
from jax import lax
from jax.experimental import pallas as pl
from jax.experimental.pallas import tpu as pltpu
from jax.sharding import PartitionSpec as P

MESH = pl.DeviceIdType.MESH
F32 = jnp.float32
BF16 = jnp.bfloat16

HD = 128
RANK = 64
CAP = 16
LANES = 128
KV_CHUNK = 4
ADAPTER_SCALING = 2.0
MASKED = -1e30


def nt_dot(a, b):
    return lax.dot_general(a, b, (((1,), (1,)), ((), ())), preferred_element_type=F32)


def tn_dot(a, b):
    return lax.dot_general(a, b, (((0,), (0,)), ((), ())), preferred_element_type=F32)


def dot(a, b):
    return jnp.dot(a, b, preferred_element_type=F32)


def iota(shape, dim):
    return lax.broadcasted_iota(jnp.int32, shape, dim)


def panel_batches(side):
    def far(v):
        return min(v, side - v)

    offsets = [(dy, dz) for dy in range(side) for dz in range(side) if dy or dz]
    batches = [[], [], []]
    for dy, dz in offsets:
        if far(dy) == far(dz):
            batches[0].append((far(dy), dy, dz))
        elif far(dy) + far(dz) == 2:
            batches[1].append((0, dy, dz))
        else:
            batches[2].append((-far(dy) - far(dz), dy, dz))
    return [[dy * side + dz for _, dy, dz in sorted(batch)] for batch in batches]


def kernel(
    n_rep, n_tp, side,
    queries, new_kv, kv_cache, lengths, ids, owners, panels, weight,
    out,
    q_own, q_in, q_rows, o_rows, fresh, cache, w_buf, pool, pack_a, pack_b, pan_a, pan_b, spread, attn, attn_back, tags, place,
    far_y, hop_y, near_y, in_y, own_y, far_z, hop_z, near_z, in_z, own_z, fwd_a, got_a, fwd_b, got_b, base,
    tag_out, tag_in, disp, work, part, part_in, shrink, delta, delta_in,
    cache_sem, load_sem, pool_sem, q_sem, pa_send, pa_recv, pb_send, pb_recv, back_send, back_recv,
    hop_y_send, hop_y_recv, y_send, y_recv, hop_z_send, hop_z_recv, z_send, z_recv, a_send, a_recv, b_send, b_recv,
    tag_send, tag_recv, disp_send, disp_recv, part_send, part_recv, shr_send, shr_recv, del_send, del_recv,
):
    steps, rows, width = out.shape
    half = rows // 2
    heads = width // HD
    per_request = 2 * heads * steps
    total_rows = steps * rows
    part_width = width // 2
    bits = n_tp.bit_length() - 1
    cap_bits = CAP.bit_length() - 1

    rep = lax.axis_index("rep")
    t = lax.axis_index("tp")
    y, z = lax.div(t, side), lax.rem(t, side)
    member, group = lax.rem(t, 2), lax.div(t, 2)
    partner = t + 1 - 2 * member
    mine = pl.multiple_of(member * half, half)
    other = pl.multiple_of((1 - member) * half, half)

    def tp_peer(k):
        dy, dz = lax.div(k, side), lax.rem(k, side)
        return lax.rem(y + dy, side) * side + lax.rem(z + dz, side)

    chip, core = lax.div(rep, 2), lax.rem(rep, 2)
    chips = n_rep // 2

    def rep_peer(k):
        m, f = lax.div(k, 2), lax.rem(k, 2)
        return lax.rem(chip + m, chips) * 2 + lax.rem(core + f, 2)

    def remote(src, dst, send, recv, device):
        return pltpu.make_async_remote_copy(
            src_ref=src, dst_ref=dst, send_sem=send, recv_sem=recv, device_id=device, device_id_type=MESH
        )

    def over(low, high, body):
        def run(k, carry):
            body(k)
            return carry

        lax.fori_loop(low, high, run, 0)

    load_q = pltpu.make_async_copy(queries.at[:, pl.ds(mine, half), :], q_own, load_sem.at[0])
    load_fresh = pltpu.make_async_copy(
        new_kv.at[:, pl.ds(mine, half), pl.ds(pl.multiple_of(group * 2 * HD, 2 * HD), 2 * HD)], fresh, load_sem.at[1]
    )
    load_w = pltpu.make_async_copy(weight, w_buf, load_sem.at[2])

    def load_cache(c):
        span = pl.ds(c * KV_CHUNK, KV_CHUNK)
        return pltpu.make_async_copy(kv_cache.at[span], cache.at[span], cache_sem.at[c])

    def load_pool(p):
        span = pl.ds(pl.multiple_of(p * width, width), width)
        return pltpu.make_async_copy(panels.at[0, span, :], pool.at[p], pool_sem.at[p])

    barrier = pltpu.get_barrier_semaphore()
    over(1, n_tp, lambda k: pl.semaphore_signal(barrier, inc=1, device_id=(rep, tp_peer(k)), device_id_type=MESH))
    over(1, n_rep, lambda k: pl.semaphore_signal(barrier, inc=1, device_id=(rep_peer(k), t), device_id_type=MESH))
    load_q.start()
    over(0, n_tp, lambda p: load_pool(p).start())
    load_fresh.start()
    over(0, half // KV_CHUNK, lambda c: load_cache(c).start())
    load_w.start()
    pl.semaphore_wait(barrier, n_tp + n_rep - 2)

    swap_q = remote(queries.at[:, pl.ds(other, half), :], q_in, q_sem.at[0], q_sem.at[1], (rep, partner))
    swap_q.start()

    half_width = width // 2
    low_half = iota((half_width, LANES), 1) < RANK

    def pack(p):
        load_pool(p).wait()
        top = pool[p, :half_width, :].astype(F32)
        bottom = pool[p, half_width:, :].astype(F32)
        pack_a[p] = jnp.where(low_half, top, pltpu.roll(bottom, RANK, 1)).astype(BF16)
        pack_b[p] = jnp.where(low_half, pltpu.roll(top, RANK, 1), bottom).astype(BF16)

    pan_cols = pl.ds(pl.multiple_of(t * LANES, LANES), LANES)

    def send_a(k):
        peer = tp_peer(k)
        return remote(pack_a.at[peer], pan_a.at[:, pan_cols], pa_send.at[k], pa_recv.at[k], (rep, peer))

    def send_b(k):
        peer = tp_peer(k)
        return remote(pack_b.at[peer], pan_b.at[:, pan_cols], pb_send.at[k], pb_recv.at[k], (rep, peer))

    pan_batches = panel_batches(side)

    def start_all(send, batch):
        for k in pan_batches[batch]:
            send(k).start()

    for k in pan_batches[0] + pan_batches[1]:
        pack(tp_peer(k))
        send_a(k).start()
    for k in pan_batches[2]:
        pack(tp_peer(k))
    pack(t)
    keep_a = pltpu.make_async_copy(pack_a.at[t], pan_a.at[:, pan_cols], load_sem.at[3])
    keep_b = pltpu.make_async_copy(pack_b.at[t], pan_b.at[:, pan_cols], load_sem.at[4])
    keep_a.start()
    keep_b.start()

    n_dest = n_rep * CAP
    n_adapters = owners.shape[1]
    diagonal = iota((rows, rows), 0) == iota((rows, rows), 1)
    earlier = jnp.where(iota((rows, rows), 1) < iota((rows, rows), 0), 1.0, 0.0).astype(BF16)
    dest = iota((rows, n_dest), 1)
    for s in range(steps):
        id_row = jnp.broadcast_to(ids[s : s + 1, :].astype(F32), (rows, rows))
        id_col = jnp.sum(jnp.where(diagonal, id_row, 0.0), axis=1, keepdims=True)
        found = iota((rows, n_adapters), 1).astype(F32) == id_col
        owner_row = jnp.broadcast_to(owners[...].astype(F32), (rows, n_adapters))
        slot = jnp.sum(jnp.where(found, owner_row, 0.0), axis=1, keepdims=True).astype(jnp.int32)
        holder = lax.shift_right_logical(slot, bits)
        goes = lax.shift_right_logical(dest, cap_bits) == holder
        rank = dot(earlier, jnp.where(goes, 1.0, 0.0).astype(BF16))
        here = goes & (rank == (dest & (CAP - 1)).astype(F32))
        place[s] = jnp.where(here, 1.0, 0.0).astype(BF16)
        tags[s] = jnp.where(iota((rows, LANES), 1) == (slot & (n_tp - 1)), 1.0, 0.0).astype(BF16)
    spread[...] = jnp.where(
        iota(spread.shape, 0) == lax.shift_right_logical(iota(spread.shape, 1), 7), 1.0, 0.0
    ).astype(BF16)

    for s in range(steps):
        sent = tn_dot(place[s], tags[s]).astype(BF16).reshape(n_rep, CAP, LANES)
        tag_out[:, s * CAP : (s + 1) * CAP, :] = sent

    def send_tag(k):
        peer = rep_peer(k)
        return remote(tag_out.at[peer], tag_in.at[rep], tag_send.at[k], tag_recv.at[k], (peer, t))

    over(1, n_rep, lambda k: send_tag(k).start())
    tag_in[rep] = tag_out[rep]

    load_q.wait()
    load_fresh.wait()
    swap_q.wait()
    for s in range(steps):
        for h in range(heads):
            cols = slice(h * HD, (h + 1) * HD)
            q_rows[pl.ds(h * steps + s, half, stride=per_request), :] = q_own[s, :, cols].astype(F32)
            q_rows[pl.ds((heads + h) * steps + s, half, stride=per_request), :] = q_in[s, :, cols].astype(F32)

    scale = 1.0 / math.sqrt(HD)

    def rows_of(i):
        return pl.ds(pl.multiple_of(i * per_request, per_request), per_request)

    def attend_chunk(c):
        load_cache(c).wait()
        block = [c * KV_CHUNK + j for j in range(KV_CHUNK)]
        step_of = iota((per_request, 1), 0) & (steps - 1)
        fresh_rows = fresh[...].reshape(steps * half, 2 * HD)
        scores, own = [], []
        for i in block:
            q = q_rows[rows_of(i), :].astype(BF16)
            scores.append(nt_dot(q, cache[i, :, :HD]))
            own.append(nt_dot(q, fresh_rows[:, :HD]))
        total = []
        for j, i in enumerate(block):
            limit = jnp.zeros((per_request, 1), jnp.int32)
            for s in range(steps):
                limit = jnp.where(step_of == s, lengths[s, mine + i], limit)
            cached = jnp.where(iota(scores[j].shape, 1) < limit, scores[j] * scale, MASKED)
            fresh_score = jnp.where(iota(own[j].shape, 1) == step_of * half + i, own[j] * scale, MASKED)
            top = jnp.maximum(
                jnp.max(cached, axis=1, keepdims=True), jnp.max(fresh_score, axis=1, keepdims=True)
            )
            cached = jnp.exp(cached - top)
            fresh_score = jnp.exp(fresh_score - top)
            total.append(jnp.sum(cached, axis=1, keepdims=True) + jnp.sum(fresh_score, axis=1, keepdims=True))
            scores[j] = cached.astype(BF16)
            own[j] = fresh_score.astype(BF16)
        for j, i in enumerate(block):
            mixed = dot(scores[j], cache[i, :, HD:]) + dot(own[j], fresh_rows[:, HD:])
            o_rows[rows_of(i), :] = mixed / total[j]

    quarter = half // 2

    def swap_back(part):
        span = pl.ds(pl.multiple_of(mine + part * quarter, quarter), quarter)
        return remote(
            attn_back.at[:, pl.ds(part * quarter, quarter), :], attn.at[:, span, :],
            back_send.at[part], back_recv.at[part], (rep, partner),
        )

    for part_of in range(2):
        chunks = quarter // KV_CHUNK
        over(part_of * chunks, (part_of + 1) * chunks, attend_chunk)
        first = part_of * quarter * per_request
        span = pl.ds(pl.multiple_of(mine + part_of * quarter, quarter), quarter)
        back = slice(part_of * quarter, (part_of + 1) * quarter)
        for s in range(steps):
            for h in range(heads):
                cols = slice(h * HD, (h + 1) * HD)
                far_heads = o_rows[pl.ds(first + (heads + h) * steps + s, quarter, stride=per_request), :]
                attn_back[s, back, cols] = far_heads.astype(BF16)
        swap_back(part_of).start()
        if part_of == 0:
            start_all(send_a, 2)
        for s in range(steps):
            for h in range(heads):
                cols = slice(h * HD, (h + 1) * HD)
                own_heads = o_rows[pl.ds(first + h * steps + s, quarter, stride=per_request), :]
                attn[s, span, cols] = own_heads.astype(BF16)
    for part_of in range(2):
        swap_back(part_of).wait_recv()

    for s in range(steps):
        span = slice(s * CAP, (s + 1) * CAP)
        routed = tn_dot(place[s], attn[s]).astype(BF16)
        disp[:, span, :] = routed.reshape(n_rep, CAP, width)

    def send_disp(k):
        peer = rep_peer(k)
        return remote(disp.at[peer], work.at[rep], disp_send.at[k], disp_recv.at[k], (peer, t))

    near_first = (0, 1, chips - 1, 2)
    for m in near_first:
        for f in range(2):
            if m or f:
                send_disp(2 * m + f).start()
    work[rep] = disp[rep]

    load_w.wait()

    def project(block, part):
        cols = pl.ds(pl.multiple_of(block * width + part * part_width, part_width), part_width)
        return dot(attn[...].reshape(total_rows, width), w_buf[:, cols])

    half_total = total_rows // 2
    halves = (slice(0, half_total), slice(half_total, total_rows))

    def at_y(d):
        return lax.rem(y + d, side) * side + z

    def at_z(d):
        return y * side + lax.rem(z + d, side)

    def hop_along_y(way, j):
        return remote(
            far_y.at[way, j], hop_y.at[way, j], hop_y_send.at[way, j], hop_y_recv.at[way, j],
            (rep, at_y((side - 1, 1)[way])),
        )

    def hop_along_z(way, j):
        return remote(
            far_z.at[way, j], hop_z.at[way, j], hop_z_send.at[way, j], hop_z_recv.at[way, j],
            (rep, at_z((side - 1, 1)[way])),
        )

    def along_y(way, j):
        return remote(
            near_y.at[way, j], in_y.at[way, j], y_send.at[way, j], y_recv.at[way, j], (rep, at_y((side - 1, 1)[way]))
        )

    def along_z(way, j):
        return remote(
            near_z.at[way, j], in_z.at[way, j], z_send.at[way, j], z_recv.at[way, j], (rep, at_z((side - 1, 1)[way]))
        )

    def far_terms(j):
        to_z = lax.rem(z + 1 + j, side)
        to_y = lax.rem(y + 1 + j, side)
        term = project(lax.rem(y + 2, side) * side + to_z, 0).astype(BF16)
        for way in range(2):
            far_y[way, j] = term[halves[way]]
            hop_along_y(way, j).start()
        term = project(to_y * side + lax.rem(z + 2, side), 1).astype(BF16)
        for way in range(2):
            far_z[way, j] = term[halves[way]]
            hop_along_z(way, j).start()

    def near_terms(j):
        to_z = lax.rem(z + 1 + j, side)
        to_y = lax.rem(y + 1 + j, side)
        for way in range(2):
            d = (side - 1, 1)[way]
            term = project(lax.rem(y + d, side) * side + to_z, 0)
            near_y[way, j, halves[1 - way], :] = term[halves[1 - way]].astype(BF16)
            hop_along_y(way, j).wait_recv()
            near_y[way, j, halves[way], :] = (term[halves[way]] + hop_y[way, j].astype(F32)).astype(BF16)
            along_y(way, j).start()
            term = project(to_y * side + lax.rem(z + d, side), 1)
            near_z[way, j, halves[1 - way], :] = term[halves[1 - way]].astype(BF16)
            hop_along_z(way, j).wait_recv()
            near_z[way, j, halves[way], :] = (term[halves[way]] + hop_z[way, j].astype(F32)).astype(BF16)
            along_z(way, j).start()
        own_y[j] = project(y * side + to_z, 0)
        own_z[j] = project(to_y * side + z, 1)

    over(0, side, far_terms)
    start_all(send_b, 0)

    work_rows = n_rep * steps * CAP
    packed_rows = work_rows // 2
    tile = 2 * steps * CAP
    low_lanes = iota((tile, LANES), 1) < RANK
    low_all = (iota((tile, n_tp * LANES), 1) & (LANES - 1)) < RANK

    def masks(source):
        return dot(tag_in[pl.ds(2 * source, 2)].reshape(tile, LANES), spread[...])

    def packed(source):
        block = lax.rem(source, chips // 2)
        return pl.ds(pl.multiple_of(block * tile, tile), tile), source >= chips // 2

    over(1, n_rep, lambda k: send_tag(k).wait_recv())
    keep_a.wait()
    over(1, n_tp, lambda k: send_a(k).wait_recv())
    for order, m in enumerate(near_first):
        for f in range(2):
            if m or f:
                send_disp(2 * m + f).wait_recv()
        source = lax.rem(chip + chips - m, chips)
        x = work[pl.ds(2 * source, 2)].reshape(tile, width)
        products = jnp.where(
            low_all, dot(x[:, :half_width], pan_a[...]), dot(x[:, half_width:], pan_a[...])
        ) * masks(source)
        total = products[:, :LANES]
        for a in range(1, n_tp):
            total = total + products[:, a * LANES : (a + 1) * LANES]
        total = total + pltpu.roll(total, RANK, 1)
        place_rows, upper = packed(source)
        if order < 2:
            part[place_rows, :] = total
        else:
            part[place_rows, :] = jnp.where(low_lanes != upper, total, part[place_rows, :])

    slab = packed_rows // n_tp

    def slab_of(device):
        return pl.ds(pl.multiple_of(device * slab, slab), slab)

    def send_part(k):
        peer = tp_peer(k)
        return remote(part.at[slab_of(peer)], part_in.at[k], part_send.at[k], part_recv.at[k], (rep, peer))

    over(1, n_tp, lambda k: send_part(k).start())
    start_all(send_b, 1)
    start_all(send_b, 2)

    def forward_y(j):
        device = (rep, y * side + lax.rem(z + 1 + j, side))
        return remote(fwd_a.at[j], got_a.at[j], a_send.at[j], a_recv.at[j], device)

    def forward_z(j):
        device = (rep, lax.rem(y + 1 + j, side) * side + z)
        return remote(fwd_b.at[j], got_b.at[j], b_send.at[j], b_recv.at[j], device)

    def gathered(own, arrived, copy, j):
        total = own[j]
        for way in range(2):
            copy(way, j).wait_recv()
            total = total + arrived[way, j].astype(F32)
        return total

    def second_stage(j):
        fwd_a[j] = gathered(own_y, in_y, along_y, j).astype(BF16)
        forward_y(j).start()
        fwd_b[j] = gathered(own_z, in_z, along_z, j).astype(BF16)
        forward_z(j).start()

    over(1, n_tp, lambda k: send_part(k).wait_recv())
    total = part[slab_of(t), :]
    for k in range(1, n_tp):
        total = total + part_in[k]
    shrink[slab_of(t), :] = total.astype(BF16)

    def send_shrink(k):
        peer = tp_peer(k)
        return remote(shrink.at[slab_of(t)], shrink.at[slab_of(t)], shr_send.at[k], shr_recv.at[k], (rep, peer))

    over(1, n_tp, lambda k: send_shrink(k).start())
    over(0, side, near_terms)

    over(1, n_tp, lambda k: send_shrink(k).wait_recv())

    keep_b.wait()
    over(1, n_tp, lambda k: send_b(k).wait_recv())

    def send_delta(k):
        peer = rep_peer(k)
        return remote(delta.at[peer], delta_in.at[rep], del_send.at[k], del_recv.at[k], (peer, t))

    for m in near_first[::-1]:
        source = lax.rem(chip + m, chips)
        place_rows, upper = packed(source)
        shrunk = shrink[place_rows, :].astype(F32)
        turned = pltpu.roll(shrunk, RANK, 1)
        in_low = jnp.where(low_lanes, jnp.where(upper, turned, shrunk), 0.0)
        in_high = jnp.where(low_lanes, 0.0, jnp.where(upper, shrunk, turned))
        mask = masks(source)
        for side_of, placed in enumerate((in_low, in_high)):
            picked = (mask * jnp.concatenate([placed] * n_tp, axis=1)).astype(BF16)
            result = nt_dot(picked, pan_b[...]).astype(BF16)
            cols = slice(side_of * half_width, (side_of + 1) * half_width)
            delta[pl.ds(2 * source, 2), :, cols] = result.reshape(2, steps * CAP, half_width)
        for f in range(2):
            if m or f:
                send_delta(2 * m + f).start()
    delta_in[rep] = delta[rep]
    over(0, side - 1, second_stage)

    last = side - 1
    base[:, :part_width] = gathered(own_y, in_y, along_y, last)
    base[:, part_width:] = gathered(own_z, in_z, along_z, last)
    for j in range(last):
        forward_y(j).wait_recv()
        base[:, :part_width] += got_a[j].astype(F32)
        forward_z(j).wait_recv()
        base[:, part_width:] += got_b[j].astype(F32)

    over(1, n_rep, lambda k: send_delta(k).wait_recv())
    for s in range(steps):
        rows_in = delta_in[:, s * CAP : (s + 1) * CAP, :].reshape(n_dest, width)
        update = dot(place[s], rows_in)
        out[s] = (base[s * rows : (s + 1) * rows, :] + ADAPTER_SCALING * update).astype(BF16)

    def drain_tp(k):
        send_a(k).wait_send()
        send_b(k).wait_send()
        send_part(k).wait_send()
        send_shrink(k).wait_send()

    def drain_rep(k):
        send_tag(k).wait_send()
        send_disp(k).wait_send()
        send_delta(k).wait_send()

    def drain_sums(j):
        for way in range(2):
            hop_along_y(way, j).wait_send()
            hop_along_z(way, j).wait_send()
            along_y(way, j).wait_send()
            along_z(way, j).wait_send()

    def drain_forward(j):
        forward_y(j).wait_send()
        forward_z(j).wait_send()

    for part_of in range(2):
        swap_back(part_of).wait_send()
    over(1, n_tp, drain_tp)
    over(1, n_rep, drain_rep)
    over(0, side, drain_sums)
    over(0, side - 1, drain_forward)


def shards(n_rep, n_tp, queries, new_kv, kv_cache, lengths, adapter_ids, owner_slot, panels, out_weight):
    side = math.isqrt(n_tp)
    steps, rows, width = queries.shape
    half = rows // 2
    heads = width // HD
    total = steps * rows
    part = width // 2
    per_request = 2 * heads * steps
    work_rows = n_rep * steps * CAP
    dma = pltpu.SemaphoreType.DMA
    vmem = pltpu.VMEM
    hop = side - 1
    scratch = [
        vmem((steps, half, width), BF16),
        vmem((steps, half, width), BF16),
        vmem((half * per_request, HD), F32),
        vmem((half * per_request, HD), F32),
        vmem((steps, half, 2 * HD), BF16),
        vmem(kv_cache.shape, BF16),
        vmem(out_weight.shape, BF16),
        vmem((n_tp, width, LANES), BF16),
        vmem((n_tp, width // 2, LANES), BF16),
        vmem((n_tp, width // 2, LANES), BF16),
        vmem((width // 2, n_tp * LANES), BF16),
        vmem((width // 2, n_tp * LANES), BF16),
        vmem((LANES, n_tp * LANES), BF16),
        vmem((steps, rows, width), BF16),
        vmem((steps, half, width), BF16),
        vmem((steps, rows, LANES), BF16),
        vmem((steps, rows, n_rep * CAP), BF16),
        vmem((2, side, total // 2, part), BF16),
        vmem((2, side, total // 2, part), BF16),
        vmem((2, side, total, part), BF16),
        vmem((2, side, total, part), BF16),
        vmem((side, total, part), F32),
        vmem((2, side, total // 2, part), BF16),
        vmem((2, side, total // 2, part), BF16),
        vmem((2, side, total, part), BF16),
        vmem((2, side, total, part), BF16),
        vmem((side, total, part), F32),
        vmem((hop, total, part), BF16),
        vmem((hop, total, part), BF16),
        vmem((hop, total, part), BF16),
        vmem((hop, total, part), BF16),
        vmem((total, width), F32),
        vmem((n_rep, steps * CAP, LANES), BF16),
        vmem((n_rep, steps * CAP, LANES), BF16),
        vmem((n_rep, steps * CAP, width), BF16),
        vmem((n_rep, steps * CAP, width), BF16),
        vmem((work_rows // 2, LANES), F32),
        vmem((n_tp, work_rows // 2 // n_tp, LANES), F32),
        vmem((work_rows // 2, LANES), BF16),
        vmem((n_rep, steps * CAP, width), BF16),
        vmem((n_rep, steps * CAP, width), BF16),
        dma((half // KV_CHUNK,)),
        dma((5,)),
        dma((n_tp,)),
        dma((2,)),
        dma((n_tp,)), dma((n_tp,)),
        dma((n_tp,)), dma((n_tp,)),
        dma((2,)), dma((2,)),
        dma((2, side)), dma((2, side)),
        dma((2, side)), dma((2, side)),
        dma((2, side)), dma((2, side)),
        dma((2, side)), dma((2, side)),
        dma((hop,)), dma((hop,)),
        dma((hop,)), dma((hop,)),
        dma((n_rep,)), dma((n_rep,)),
        dma((n_rep,)), dma((n_rep,)),
        dma((n_tp,)), dma((n_tp,)),
        dma((n_tp,)), dma((n_tp,)),
        dma((n_rep,)), dma((n_rep,)),
    ]
    hbm = pl.BlockSpec(memory_space=pl.ANY)
    in_vmem = pl.BlockSpec(memory_space=pltpu.VMEM)
    in_smem = pl.BlockSpec(memory_space=pltpu.SMEM)
    return pl.pallas_call(
        functools.partial(kernel, n_rep, n_tp, side),
        out_shape=jax.ShapeDtypeStruct(queries.shape, BF16),
        in_specs=[hbm, hbm, hbm, in_smem, in_vmem, in_vmem, hbm, hbm],
        out_specs=in_vmem,
        scratch_shapes=scratch,
        compiler_params=pltpu.CompilerParams(
            collective_id=0, has_side_effects=True, vmem_limit_bytes=56 * 1024 * 1024
        ),
        cost_estimate=pl.CostEstimate(
            flops=5_000_000_000, bytes_accessed=20_000_000, transcendentals=600_000
        ),
    )(queries, new_kv, kv_cache, lengths, adapter_ids, owner_slot.reshape(1, -1), panels, out_weight)


def solution(mesh):
    placed = (
        P(None, "rep", "tp"),
        P(None, "rep", None),
        P("rep", None, "tp"),
        P(None, "rep"),
        P(None, "rep"),
        P(),
        P(("rep", "tp"), None, None),
        P("tp", None),
    )
    return jax.shard_map(
        functools.partial(shards, mesh.shape["rep"], mesh.shape["tp"]),
        mesh=mesh, in_specs=placed, out_specs=P(None, "rep", "tp"), check_vma=False,
    )
```

time: 88.9 us -> 75.3 us (0.85)
  Pallas kernels: 85.7 us -> 72.6 us
    pallas_call x1, Pallas kernels: 85.7 us -> 72.6 us  [shards(): pl.pallas_call(functools.partial(kernel, n_rep, n_tp, side), out_shape=ja...]
where the time goes in v2:
time: 75.3 us; the launch traced here: 74.3 us
  Pallas kernels  72.6 us (96%)
  local copies, waits for them, and re-layouts  1.67 us (2%)
    pallas_call x1, Pallas kernels, shards(): pl.pallas_call(functools.partial(kernel, n_rep, n_tp, side), out_shape=ja...  72.6 us
    unnamed x1, local copies, waits for them, and re-layouts  1.67 us

profile of v2, /device:TPU:0, one launch (start us, length us, event | category | flops | bytes accessed | tf_op | source)
XLA Modules:
  0.0 74.3 jit_solution(6362940385799675877)
XLA Ops:
  0.0 72.6 %shard_map.82 = bf16[4,64,512]{2,1,0:T(8,128)(2,1)} custom-call(bf16[4,64,512]{2,1,0:T(8,128)(2,1)} %queries.1, bf16[4,64,2048]{2,1,0:T(8,128)(2,1)} %new_kv.1, bf16[32,512,256]{2,1,0:T(8,128)(2,1)} %kv_cache.1, s32[4,64]{1,0:T(4,128)} %lengths.1, s32[4,64]{1,0:T(4,128)} %ids.1, s32[1,128]{1,0:T(1,128)} %bitcast.1, bf16[1,8192,128]{2,1,0:T(8,128)(2,1)} %panels.1, ...), custom_call_target="tpu_custom_call" | custom-call | flops 5000000000 | bytes 20000000 | tf_op jit(solution)/shard_map/pallas_call | solution.py:594
  72.6 1.7 %copy.10 = bf16[4,64,512]{2,1,0:T(8,128)(2,1)} copy(bf16[4,64,512]{2,1,0:T(8,128)(2,1)} %shard_map.82) | data formatting | bytes 524288

commit v3 on v2

--- a/solution.py
+++ b/solution.py
@@ -16,7 +16,7 @@
 RANK = 64
 CAP = 16
 LANES = 128
-KV_CHUNK = 4
+KV_CHUNK = 8
 ADAPTER_SCALING = 2.0
 MASKED = -1e30
 
@@ -97,6 +97,9 @@
             src_ref=src, dst_ref=dst, send_sem=send, recv_sem=recv, device_id=device, device_id_type=MESH
         )
 
+    def landed(region, sem):
+        pltpu.make_async_copy(region, region, sem.at[0]).wait()
+
     def over(low, high, body):
         def run(k, carry):
             body(k)
@@ -119,18 +122,15 @@
         return pltpu.make_async_copy(panels.at[0, span, :], pool.at[p], pool_sem.at[p])
 
     barrier = pltpu.get_barrier_semaphore()
-    over(1, n_tp, lambda k: pl.semaphore_signal(barrier, inc=1, device_id=(rep, tp_peer(k)), device_id_type=MESH))
-    over(1, n_rep, lambda k: pl.semaphore_signal(barrier, inc=1, device_id=(rep_peer(k), t), device_id_type=MESH))
+    for k in range(1, n_tp):
+        pl.semaphore_signal(barrier, inc=1, device_id=(rep, tp_peer(k)), device_id_type=MESH)
+    for k in range(1, n_rep):
+        pl.semaphore_signal(barrier, inc=1, device_id=(rep_peer(k), t), device_id_type=MESH)
+    over(0, n_tp, lambda p: load_pool(p).start())
     load_q.start()
-    over(0, n_tp, lambda p: load_pool(p).start())
     load_fresh.start()
     over(0, half // KV_CHUNK, lambda c: load_cache(c).start())
     load_w.start()
-    pl.semaphore_wait(barrier, n_tp + n_rep - 2)
-
-    swap_q = remote(queries.at[:, pl.ds(other, half), :], q_in, q_sem.at[0], q_sem.at[1], (rep, partner))
-    swap_q.start()
-
     half_width = width // 2
     low_half = iota((half_width, LANES), 1) < RANK
 
@@ -145,24 +145,28 @@
 
     def send_a(k):
         peer = tp_peer(k)
-        return remote(pack_a.at[peer], pan_a.at[:, pan_cols], pa_send.at[k], pa_recv.at[k], (rep, peer))
+        return remote(pack_a.at[peer], pan_a.at[:, pan_cols], pa_send.at[0], pa_recv.at[0], (rep, peer))
 
     def send_b(k):
         peer = tp_peer(k)
-        return remote(pack_b.at[peer], pan_b.at[:, pan_cols], pb_send.at[k], pb_recv.at[k], (rep, peer))
+        return remote(pack_b.at[peer], pan_b.at[:, pan_cols], pb_send.at[0], pb_recv.at[0], (rep, peer))
 
     pan_batches = panel_batches(side)
+    spread_out = pan_batches[0] + pan_batches[1] + pan_batches[2]
 
     def start_all(send, batch):
         for k in pan_batches[batch]:
             send(k).start()
 
-    for k in pan_batches[0] + pan_batches[1]:
-        pack(tp_peer(k))
+    over(0, n_tp, pack)
+
+    pl.semaphore_wait(barrier, n_tp + n_rep - 2)
+
+    swap_q = remote(queries.at[:, pl.ds(other, half), :], q_in, q_sem.at[0], q_sem.at[1], (rep, partner))
+    swap_q.start()
+
+    for k in pan_batches[0] + pan_batches[1] + pan_batches[2]:
         send_a(k).start()
-    for k in pan_batches[2]:
-        pack(tp_peer(k))
-    pack(t)
     keep_a = pltpu.make_async_copy(pack_a.at[t], pan_a.at[:, pan_cols], load_sem.at[3])
     keep_b = pltpu.make_async_copy(pack_b.at[t], pan_b.at[:, pan_cols], load_sem.at[4])
     keep_a.start()
@@ -195,9 +199,10 @@
 
     def send_tag(k):
         peer = rep_peer(k)
-        return remote(tag_out.at[peer], tag_in.at[rep], tag_send.at[k], tag_recv.at[k], (peer, t))
-
-    over(1, n_rep, lambda k: send_tag(k).start())
+        return remote(tag_out.at[peer], tag_in.at[rep], tag_send.at[0], tag_recv.at[0], (peer, t))
+
+    for k in range(1, n_rep):
+        send_tag(k).start()
     tag_in[rep] = tag_out[rep]
 
     load_q.wait()
@@ -264,8 +269,6 @@
                 far_heads = o_rows[pl.ds(first + (heads + h) * steps + s, quarter, stride=per_request), :]
                 attn_back[s, back, cols] = far_heads.astype(BF16)
         swap_back(part_of).start()
-        if part_of == 0:
-            start_all(send_a, 2)
         for s in range(steps):
             for h in range(heads):
                 cols = slice(h * HD, (h + 1) * HD)
@@ -281,7 +284,7 @@
 
     def send_disp(k):
         peer = rep_peer(k)
-        return remote(disp.at[peer], work.at[rep], disp_send.at[k], disp_recv.at[k], (peer, t))
+        return remote(disp.at[peer], work.at[rep], disp_send.at[0], disp_recv.at[k], (peer, t))
 
     near_first = (0, 1, chips - 1, 2)
     for m in near_first:
@@ -307,24 +310,24 @@
 
     def hop_along_y(way, j):
         return remote(
-            far_y.at[way, j], hop_y.at[way, j], hop_y_send.at[way, j], hop_y_recv.at[way, j],
+            far_y.at[way, j], hop_y.at[way, j], hop_y_send.at[0], hop_y_recv.at[way, j],
             (rep, at_y((side - 1, 1)[way])),
         )
 
     def hop_along_z(way, j):
         return remote(
-            far_z.at[way, j], hop_z.at[way, j], hop_z_send.at[way, j], hop_z_recv.at[way, j],
+            far_z.at[way, j], hop_z.at[way, j], hop_z_send.at[0], hop_z_recv.at[way, j],
             (rep, at_z((side - 1, 1)[way])),
         )
 
     def along_y(way, j):
         return remote(
-            near_y.at[way, j], in_y.at[way, j], y_send.at[way, j], y_recv.at[way, j], (rep, at_y((side - 1, 1)[way]))
+            near_y.at[way, j], in_y.at[way, j], y_send.at[0], y_recv.at[way, j], (rep, at_y((side - 1, 1)[way]))
         )
 
     def along_z(way, j):
         return remote(
-            near_z.at[way, j], in_z.at[way, j], z_send.at[way, j], z_recv.at[way, j], (rep, at_z((side - 1, 1)[way]))
+            near_z.at[way, j], in_z.at[way, j], z_send.at[0], z_recv.at[way, j], (rep, at_z((side - 1, 1)[way]))
         )
 
     def far_terms(j):
@@ -373,9 +376,9 @@
         block = lax.rem(source, chips // 2)
         return pl.ds(pl.multiple_of(block * tile, tile), tile), source >= chips // 2
 
-    over(1, n_rep, lambda k: send_tag(k).wait_recv())
+    landed(tag_in.at[pl.ds(0, n_rep - 1)], tag_recv)
     keep_a.wait()
-    over(1, n_tp, lambda k: send_a(k).wait_recv())
+    landed(pan_a.at[:, pl.ds(0, (n_tp - 1) * LANES)], pa_recv)
     for order, m in enumerate(near_first):
         for f in range(2):
             if m or f:
@@ -402,19 +405,20 @@
 
     def send_part(k):
         peer = tp_peer(k)
-        return remote(part.at[slab_of(peer)], part_in.at[k], part_send.at[k], part_recv.at[k], (rep, peer))
-
-    over(1, n_tp, lambda k: send_part(k).start())
+        return remote(part.at[slab_of(peer)], part_in.at[k], part_send.at[0], part_recv.at[0], (rep, peer))
+
+    for k in spread_out:
+        send_part(k).start()
     start_all(send_b, 1)
     start_all(send_b, 2)
 
     def forward_y(j):
         device = (rep, y * side + lax.rem(z + 1 + j, side))
-        return remote(fwd_a.at[j], got_a.at[j], a_send.at[j], a_recv.at[j], device)
+        return remote(fwd_a.at[j], got_a.at[j], a_send.at[0], a_recv.at[j], device)
 
     def forward_z(j):
         device = (rep, lax.rem(y + 1 + j, side) * side + z)
-        return remote(fwd_b.at[j], got_b.at[j], b_send.at[j], b_recv.at[j], device)
+        return remote(fwd_b.at[j], got_b.at[j], b_send.at[0], b_recv.at[j], device)
 
     def gathered(own, arrived, copy, j):
         total = own[j]
@@ -429,7 +433,7 @@
         fwd_b[j] = gathered(own_z, in_z, along_z, j).astype(BF16)
         forward_z(j).start()
 
-    over(1, n_tp, lambda k: send_part(k).wait_recv())
+    landed(part_in.at[pl.ds(1, n_tp - 1)], part_recv)
     total = part[slab_of(t), :]
     for k in range(1, n_tp):
         total = total + part_in[k]
@@ -437,19 +441,20 @@
 
     def send_shrink(k):
         peer = tp_peer(k)
-        return remote(shrink.at[slab_of(t)], shrink.at[slab_of(t)], shr_send.at[k], shr_recv.at[k], (rep, peer))
-
-    over(1, n_tp, lambda k: send_shrink(k).start())
+        return remote(shrink.at[slab_of(t)], shrink.at[slab_of(t)], shr_send.at[0], shr_recv.at[0], (rep, peer))
+
+    for k in spread_out:
+        send_shrink(k).start()
     over(0, side, near_terms)
 
-    over(1, n_tp, lambda k: send_shrink(k).wait_recv())
+    landed(shrink.at[pl.ds(0, (n_tp - 1) * slab)], shr_recv)
 
     keep_b.wait()
-    over(1, n_tp, lambda k: send_b(k).wait_recv())
+    landed(pan_b.at[:, pl.ds(0, (n_tp - 1) * LANES)], pb_recv)
 
     def send_delta(k):
         peer = rep_peer(k)
-        return remote(delta.at[peer], delta_in.at[rep], del_send.at[k], del_recv.at[k], (peer, t))
+        return remote(delta.at[peer], delta_in.at[rep], del_send.at[0], del_recv.at[0], (peer, t))
 
     for m in near_first[::-1]:
         source = lax.rem(chip + m, chips)
@@ -479,40 +484,27 @@
         forward_z(j).wait_recv()
         base[:, part_width:] += got_b[j].astype(F32)
 
-    over(1, n_rep, lambda k: send_delta(k).wait_recv())
+    landed(delta_in.at[pl.ds(0, n_rep - 1)], del_recv)
     for s in range(steps):
         rows_in = delta_in[:, s * CAP : (s + 1) * CAP, :].reshape(n_dest, width)
         update = dot(place[s], rows_in)
         out[s] = (base[s * rows : (s + 1) * rows, :] + ADAPTER_SCALING * update).astype(BF16)
 
-    def drain_tp(k):
-        send_a(k).wait_send()
-        send_b(k).wait_send()
-        send_part(k).wait_send()
-        send_shrink(k).wait_send()
-
-    def drain_rep(k):
-        send_tag(k).wait_send()
-        send_disp(k).wait_send()
-        send_delta(k).wait_send()
-
-    def drain_sums(j):
-        for way in range(2):
-            hop_along_y(way, j).wait_send()
-            hop_along_z(way, j).wait_send()
-            along_y(way, j).wait_send()
-            along_z(way, j).wait_send()
-
-    def drain_forward(j):
-        forward_y(j).wait_send()
-        forward_z(j).wait_send()
-
     for part_of in range(2):
         swap_back(part_of).wait_send()
-    over(1, n_tp, drain_tp)
-    over(1, n_rep, drain_rep)
-    over(0, side, drain_sums)
-    over(0, side - 1, drain_forward)
+    landed(pack_a.at[pl.ds(0, n_tp - 1)], pa_send)
+    landed(pack_b.at[pl.ds(0, n_tp - 1)], pb_send)
+    landed(tag_out.at[pl.ds(0, n_rep - 1)], tag_send)
+    landed(disp.at[pl.ds(0, n_rep - 1)], disp_send)
+    landed(part_in.at[pl.ds(1, n_tp - 1)], part_send)
+    landed(shrink.at[pl.ds(0, (n_tp - 1) * slab)], shr_send)
+    landed(delta.at[pl.ds(0, n_rep - 1)], del_send)
+    landed(far_y, hop_y_send)
+    landed(far_z, hop_z_send)
+    landed(near_y, y_send)
+    landed(near_z, z_send)
+    landed(fwd_a, a_send)
+    landed(fwd_b, b_send)
 
 
 def shards(n_rep, n_tp, queries, new_kv, kv_cache, lengths, adapter_ids, owner_slot, panels, out_weight):
@@ -573,20 +565,20 @@
         dma((5,)),
         dma((n_tp,)),
         dma((2,)),
-        dma((n_tp,)), dma((n_tp,)),
-        dma((n_tp,)), dma((n_tp,)),
+        dma((1,)), dma((1,)),
+        dma((1,)), dma((1,)),
         dma((2,)), dma((2,)),
-        dma((2, side)), dma((2, side)),
-        dma((2, side)), dma((2, side)),
-        dma((2, side)), dma((2, side)),
-        dma((2, side)), dma((2, side)),
-        dma((hop,)), dma((hop,)),
-        dma((hop,)), dma((hop,)),
-        dma((n_rep,)), dma((n_rep,)),
-        dma((n_rep,)), dma((n_rep,)),
-        dma((n_tp,)), dma((n_tp,)),
-        dma((n_tp,)), dma((n_tp,)),
-        dma((n_rep,)), dma((n_rep,)),
+        dma((1,)), dma((2, side)),
+        dma((1,)), dma((2, side)),
+        dma((1,)), dma((2, side)),
+        dma((1,)), dma((2, side)),
+        dma((1,)), dma((hop,)),
+        dma((1,)), dma((hop,)),
+        dma((1,)), dma((1,)),
+        dma((1,)), dma((n_rep,)),
+        dma((1,)), dma((1,)),
+        dma((1,)), dma((1,)),
+        dma((1,)), dma((1,)),
     ]
     hbm = pl.BlockSpec(memory_space=pl.ANY)
     in_vmem = pl.BlockSpec(memory_space=pltpu.VMEM)

time: 75.3 us -> 70.6 us (0.938); the launches traced: 74.3 us -> 70.5 us
  Pallas kernels: 72.6 us -> 68.8 us
    pallas_call x1, Pallas kernels: 72.6 us -> 68.8 us  [shards(): pl.pallas_call(functools.partial(kernel, n_rep, n_tp, side), out_shape=ja...]
where the time goes in v3:
time: 70.6 us; the launch traced here: 70.5 us
  Pallas kernels  68.8 us (97%)
  local copies, waits for them, and re-layouts  1.67 us (2%)
    pallas_call x1, Pallas kernels, shards(): pl.pallas_call(functools.partial(kernel, n_rep, n_tp, side), out_shape=ja...  68.8 us
    unnamed x1, local copies, waits for them, and re-layouts  1.67 us

profile of v3, /device:TPU:0, one launch (start us, length us, event | category | flops | bytes accessed | tf_op | source)
XLA Modules:
  0.0 70.5 jit_solution(11459036697013036021)
XLA Ops:
  0.0 68.8 %shard_map.82 = bf16[4,64,512]{2,1,0:T(8,128)(2,1)} custom-call(bf16[4,64,512]{2,1,0:T(8,128)(2,1)} %queries.1, bf16[4,64,2048]{2,1,0:T(8,128)(2,1)} %new_kv.1, bf16[32,512,256]{2,1,0:T(8,128)(2,1)} %kv_cache.1, s32[4,64]{1,0:T(4,128)} %lengths.1, s32[4,64]{1,0:T(4,128)} %ids.1, s32[1,128]{1,0:T(1,128)} %bitcast.1, bf16[1,8192,128]{2,1,0:T(8,128)(2,1)} %panels.1, ...), custom_call_target="tpu_custom_call" | custom-call | flops 5000000000 | bytes 20000000 | tf_op jit(solution)/shard_map/pallas_call | solution.py:586
  68.8 1.7 %copy.10 = bf16[4,64,512]{2,1,0:T(8,128)(2,1)} copy(bf16[4,64,512]{2,1,0:T(8,128)(2,1)} %shard_map.82) | data formatting | bytes 524288

commit v4 on v3

--- a/solution.py
+++ b/solution.py
@@ -60,7 +60,7 @@
     q_own, q_in, q_rows, o_rows, fresh, cache, w_buf, pool, pack_a, pack_b, pan_a, pan_b, spread, attn, attn_back, tags, place,
     far_y, hop_y, near_y, in_y, own_y, far_z, hop_z, near_z, in_z, own_z, fwd_a, got_a, fwd_b, got_b, base,
     tag_out, tag_in, disp, work, part, part_in, shrink, delta, delta_in,
-    cache_sem, load_sem, pool_sem, q_sem, pa_send, pa_recv, pb_send, pb_recv, back_send, back_recv,
+    cache_sem, load_sem, pool_sem, q_send, q_recv, pa_send, pa_recv, pb_send, pb_recv, back_send, back_recv,
     hop_y_send, hop_y_recv, y_send, y_recv, hop_z_send, hop_z_recv, z_send, z_recv, a_send, a_recv, b_send, b_recv,
     tag_send, tag_recv, disp_send, disp_recv, part_send, part_recv, shr_send, shr_recv, del_send, del_recv,
 ):
@@ -130,7 +130,6 @@
     load_q.start()
     load_fresh.start()
     over(0, half // KV_CHUNK, lambda c: load_cache(c).start())
-    load_w.start()
     half_width = width // 2
     low_half = iota((half_width, LANES), 1) < RANK
 
@@ -162,11 +161,17 @@
 
     pl.semaphore_wait(barrier, n_tp + n_rep - 2)
 
-    swap_q = remote(queries.at[:, pl.ds(other, half), :], q_in, q_sem.at[0], q_sem.at[1], (rep, partner))
-    swap_q.start()
-
-    for k in pan_batches[0] + pan_batches[1] + pan_batches[2]:
-        send_a(k).start()
+    def swap_q(part):
+        span = pl.ds(pl.multiple_of(other + part * (half // 2), half // 2), half // 2)
+        here = pl.ds(part * (half // 2), half // 2)
+        return remote(queries.at[:, span, :], q_in.at[:, here, :], q_send.at[part], q_recv.at[part], (rep, partner))
+
+    for part_of in range(2):
+        swap_q(part_of).start()
+    load_w.start()
+
+    start_all(send_a, 0)
+    start_all(send_a, 1)
     keep_a = pltpu.make_async_copy(pack_a.at[t], pan_a.at[:, pan_cols], load_sem.at[3])
     keep_b = pltpu.make_async_copy(pack_b.at[t], pan_b.at[:, pan_cols], load_sem.at[4])
     keep_a.start()
@@ -207,12 +212,10 @@
 
     load_q.wait()
     load_fresh.wait()
-    swap_q.wait()
     for s in range(steps):
         for h in range(heads):
             cols = slice(h * HD, (h + 1) * HD)
             q_rows[pl.ds(h * steps + s, half, stride=per_request), :] = q_own[s, :, cols].astype(F32)
-            q_rows[pl.ds((heads + h) * steps + s, half, stride=per_request), :] = q_in[s, :, cols].astype(F32)
 
     scale = 1.0 / math.sqrt(HD)
 
@@ -258,6 +261,12 @@
         )
 
     for part_of in range(2):
+        swap_q(part_of).wait()
+        for s in range(steps):
+            for h in range(heads):
+                to = part_of * quarter * per_request + (heads + h) * steps + s
+                arrived = q_in[s, part_of * quarter : (part_of + 1) * quarter, h * HD : (h + 1) * HD]
+                q_rows[pl.ds(to, quarter, stride=per_request), :] = arrived.astype(F32)
         chunks = quarter // KV_CHUNK
         over(part_of * chunks, (part_of + 1) * chunks, attend_chunk)
         first = part_of * quarter * per_request
@@ -274,6 +283,7 @@
                 cols = slice(h * HD, (h + 1) * HD)
                 own_heads = o_rows[pl.ds(first + h * steps + s, quarter, stride=per_request), :]
                 attn[s, span, cols] = own_heads.astype(BF16)
+    start_all(send_a, 2)
     for part_of in range(2):
         swap_back(part_of).wait_recv()
 
@@ -478,17 +488,20 @@
     last = side - 1
     base[:, :part_width] = gathered(own_y, in_y, along_y, last)
     base[:, part_width:] = gathered(own_z, in_z, along_z, last)
-    for j in range(last):
-        forward_y(j).wait_recv()
-        base[:, :part_width] += got_a[j].astype(F32)
-        forward_z(j).wait_recv()
-        base[:, part_width:] += got_b[j].astype(F32)
-
     landed(delta_in.at[pl.ds(0, n_rep - 1)], del_recv)
     for s in range(steps):
         rows_in = delta_in[:, s * CAP : (s + 1) * CAP, :].reshape(n_dest, width)
-        update = dot(place[s], rows_in)
-        out[s] = (base[s * rows : (s + 1) * rows, :] + ADAPTER_SCALING * update).astype(BF16)
+        base[s * rows : (s + 1) * rows, :] += ADAPTER_SCALING * dot(place[s], rows_in)
+    for j in range(last):
+        forward_y(j).wait_recv()
+        forward_z(j).wait_recv()
+    for s in range(steps):
+        span = slice(s * rows, (s + 1) * rows)
+        for cols, got in ((slice(0, part_width), got_a), (slice(part_width, width), got_b)):
+            total = base[span, cols]
+            for j in range(last):
+                total = total + got[j, span, :].astype(F32)
+            out[s, :, cols] = total.astype(BF16)
 
     for part_of in range(2):
         swap_back(part_of).wait_send()
@@ -564,7 +577,7 @@
         dma((half // KV_CHUNK,)),
         dma((5,)),
         dma((n_tp,)),
-        dma((2,)),
+        dma((2,)), dma((2,)),
         dma((1,)), dma((1,)),
         dma((1,)), dma((1,)),
         dma((2,)), dma((2,)),

time: 70.6 us -> 68.5 us (0.970)
  Pallas kernels: 68.8 us -> 66.7 us
    pallas_call x1, Pallas kernels: 68.8 us -> 66.7 us  [shards(): pl.pallas_call(functools.partial(kernel, n_rep, n_tp, side), out_shape=ja...]
where the time goes in v4:
time: 68.5 us; the launch traced here: 68.4 us
  Pallas kernels  66.7 us (97%)
  local copies, waits for them, and re-layouts  1.67 us (2%)
    pallas_call x1, Pallas kernels, shards(): pl.pallas_call(functools.partial(kernel, n_rep, n_tp, side), out_shape=ja...  66.7 us
    unnamed x1, local copies, waits for them, and re-layouts  1.67 us

profile of v4, /device:TPU:0, one launch (start us, length us, event | category | flops | bytes accessed | tf_op | source)
XLA Modules:
  0.0 68.4 jit_solution(15662095865653706222)
XLA Ops:
  0.0 66.7 %shard_map.82 = bf16[4,64,512]{2,1,0:T(8,128)(2,1)} custom-call(bf16[4,64,512]{2,1,0:T(8,128)(2,1)} %queries.1, bf16[4,64,2048]{2,1,0:T(8,128)(2,1)} %new_kv.1, bf16[32,512,256]{2,1,0:T(8,128)(2,1)} %kv_cache.1, s32[4,64]{1,0:T(4,128)} %lengths.1, s32[4,64]{1,0:T(4,128)} %ids.1, s32[1,128]{1,0:T(1,128)} %bitcast.1, bf16[1,8192,128]{2,1,0:T(8,128)(2,1)} %panels.1, ...), custom_call_target="tpu_custom_call" | custom-call | flops 5000000000 | bytes 20000000 | tf_op jit(solution)/shard_map/pallas_call | solution.py:599
  66.7 1.7 %copy.10 = bf16[4,64,512]{2,1,0:T(8,128)(2,1)} copy(bf16[4,64,512]{2,1,0:T(8,128)(2,1)} %shard_map.82) | data formatting | bytes 524288

commit v5 on v4

--- a/solution.py
+++ b/solution.py
@@ -122,7 +122,7 @@
         return pltpu.make_async_copy(panels.at[0, span, :], pool.at[p], pool_sem.at[p])
 
     barrier = pltpu.get_barrier_semaphore()
-    for k in range(1, n_tp):
+    for k in sorted(range(1, n_tp), key=lambda k: -min(k // side, side - k // side) - min(k % side, side - k % side)):
         pl.semaphore_signal(barrier, inc=1, device_id=(rep, tp_peer(k)), device_id_type=MESH)
     for k in range(1, n_rep):
         pl.semaphore_signal(barrier, inc=1, device_id=(rep_peer(k), t), device_id_type=MESH)
@@ -176,39 +176,6 @@
     keep_b = pltpu.make_async_copy(pack_b.at[t], pan_b.at[:, pan_cols], load_sem.at[4])
     keep_a.start()
     keep_b.start()
-
-    n_dest = n_rep * CAP
-    n_adapters = owners.shape[1]
-    diagonal = iota((rows, rows), 0) == iota((rows, rows), 1)
-    earlier = jnp.where(iota((rows, rows), 1) < iota((rows, rows), 0), 1.0, 0.0).astype(BF16)
-    dest = iota((rows, n_dest), 1)
-    for s in range(steps):
-        id_row = jnp.broadcast_to(ids[s : s + 1, :].astype(F32), (rows, rows))
-        id_col = jnp.sum(jnp.where(diagonal, id_row, 0.0), axis=1, keepdims=True)
-        found = iota((rows, n_adapters), 1).astype(F32) == id_col
-        owner_row = jnp.broadcast_to(owners[...].astype(F32), (rows, n_adapters))
-        slot = jnp.sum(jnp.where(found, owner_row, 0.0), axis=1, keepdims=True).astype(jnp.int32)
-        holder = lax.shift_right_logical(slot, bits)
-        goes = lax.shift_right_logical(dest, cap_bits) == holder
-        rank = dot(earlier, jnp.where(goes, 1.0, 0.0).astype(BF16))
-        here = goes & (rank == (dest & (CAP - 1)).astype(F32))
-        place[s] = jnp.where(here, 1.0, 0.0).astype(BF16)
-        tags[s] = jnp.where(iota((rows, LANES), 1) == (slot & (n_tp - 1)), 1.0, 0.0).astype(BF16)
-    spread[...] = jnp.where(
-        iota(spread.shape, 0) == lax.shift_right_logical(iota(spread.shape, 1), 7), 1.0, 0.0
-    ).astype(BF16)
-
-    for s in range(steps):
-        sent = tn_dot(place[s], tags[s]).astype(BF16).reshape(n_rep, CAP, LANES)
-        tag_out[:, s * CAP : (s + 1) * CAP, :] = sent
-
-    def send_tag(k):
-        peer = rep_peer(k)
-        return remote(tag_out.at[peer], tag_in.at[rep], tag_send.at[0], tag_recv.at[0], (peer, t))
-
-    for k in range(1, n_rep):
-        send_tag(k).start()
-    tag_in[rep] = tag_out[rep]
 
     load_q.wait()
     load_fresh.wait()
@@ -270,7 +237,6 @@
         chunks = quarter // KV_CHUNK
         over(part_of * chunks, (part_of + 1) * chunks, attend_chunk)
         first = part_of * quarter * per_request
-        span = pl.ds(pl.multiple_of(mine + part_of * quarter, quarter), quarter)
         back = slice(part_of * quarter, (part_of + 1) * quarter)
         for s in range(steps):
             for h in range(heads):
@@ -278,12 +244,46 @@
                 far_heads = o_rows[pl.ds(first + (heads + h) * steps + s, quarter, stride=per_request), :]
                 attn_back[s, back, cols] = far_heads.astype(BF16)
         swap_back(part_of).start()
-        for s in range(steps):
-            for h in range(heads):
-                cols = slice(h * HD, (h + 1) * HD)
-                own_heads = o_rows[pl.ds(first + h * steps + s, quarter, stride=per_request), :]
-                attn[s, span, cols] = own_heads.astype(BF16)
-    start_all(send_a, 2)
+    for k in pan_batches[2][::-1]:
+        send_a(k).start()
+    for s in range(steps):
+        for h in range(heads):
+            cols = slice(h * HD, (h + 1) * HD)
+            own_heads = o_rows[pl.ds(h * steps + s, half, stride=per_request), :]
+            attn[s, pl.ds(mine, half), cols] = own_heads.astype(BF16)
+    n_dest = n_rep * CAP
+    n_adapters = owners.shape[1]
+    diagonal = iota((rows, rows), 0) == iota((rows, rows), 1)
+    earlier = jnp.where(iota((rows, rows), 1) < iota((rows, rows), 0), 1.0, 0.0).astype(BF16)
+    dest = iota((rows, n_dest), 1)
+    for s in range(steps):
+        id_row = jnp.broadcast_to(ids[s : s + 1, :].astype(F32), (rows, rows))
+        id_col = jnp.sum(jnp.where(diagonal, id_row, 0.0), axis=1, keepdims=True)
+        found = iota((rows, n_adapters), 1).astype(F32) == id_col
+        owner_row = jnp.broadcast_to(owners[...].astype(F32), (rows, n_adapters))
+        slot = jnp.sum(jnp.where(found, owner_row, 0.0), axis=1, keepdims=True).astype(jnp.int32)
+        holder = lax.shift_right_logical(slot, bits)
+        goes = lax.shift_right_logical(dest, cap_bits) == holder
+        rank = dot(earlier, jnp.where(goes, 1.0, 0.0).astype(BF16))
+        here = goes & (rank == (dest & (CAP - 1)).astype(F32))
+        place[s] = jnp.where(here, 1.0, 0.0).astype(BF16)
+        tags[s] = jnp.where(iota((rows, LANES), 1) == (slot & (n_tp - 1)), 1.0, 0.0).astype(BF16)
+    spread[...] = jnp.where(
+        iota(spread.shape, 0) == lax.shift_right_logical(iota(spread.shape, 1), 7), 1.0, 0.0
+    ).astype(BF16)
+
+    for s in range(steps):
+        sent = tn_dot(place[s], tags[s]).astype(BF16).reshape(n_rep, CAP, LANES)
+        tag_out[:, s * CAP : (s + 1) * CAP, :] = sent
+
+    def send_tag(k):
+        peer = rep_peer(k)
+        return remote(tag_out.at[peer], tag_in.at[rep], tag_send.at[0], tag_recv.at[0], (peer, t))
+
+    for k in range(1, n_rep):
+        send_tag(k).start()
+    tag_in[rep] = tag_out[rep]
+
     for part_of in range(2):
         swap_back(part_of).wait_recv()
 

time: 68.5 us -> 67.4 us (0.984)
  Pallas kernels: 66.7 us -> 65.4 us
    pallas_call x1, Pallas kernels: 66.7 us -> 65.4 us  [shards(): pl.pallas_call(functools.partial(kernel, n_rep, n_tp, side), out_shape=ja...]
where the time goes in v5:
time: 67.4 us; the launch traced here: 67 us
  Pallas kernels  65.4 us (97%)
  local copies, waits for them, and re-layouts  1.67 us (2%)
    pallas_call x1, Pallas kernels, shards(): pl.pallas_call(functools.partial(kernel, n_rep, n_tp, side), out_shape=ja...  65.4 us
    unnamed x1, local copies, waits for them, and re-layouts  1.67 us

profile of v5, /device:TPU:0, one launch (start us, length us, event | category | flops | bytes accessed | tf_op | source)
XLA Modules:
  0.0 67.0 jit_solution(974646423185060246)
XLA Ops:
  0.0 65.4 %shard_map.82 = bf16[4,64,512]{2,1,0:T(8,128)(2,1)} custom-call(bf16[4,64,512]{2,1,0:T(8,128)(2,1)} %queries.1, bf16[4,64,2048]{2,1,0:T(8,128)(2,1)} %new_kv.1, bf16[32,512,256]{2,1,0:T(8,128)(2,1)} %kv_cache.1, s32[4,64]{1,0:T(4,128)} %lengths.1, s32[4,64]{1,0:T(4,128)} %ids.1, s32[1,128]{1,0:T(1,128)} %bitcast.1, bf16[1,8192,128]{2,1,0:T(8,128)(2,1)} %panels.1, ...), custom_call_target="tpu_custom_call" | custom-call | flops 5000000000 | bytes 20000000 | tf_op jit(solution)/shard_map/pallas_call | solution.py:599
  65.4 1.7 %copy.10 = bf16[4,64,512]{2,1,0:T(8,128)(2,1)} copy(bf16[4,64,512]{2,1,0:T(8,128)(2,1)} %shard_map.82) | data formatting | bytes 524288

commit v6 on v5

--- a/solution.py
+++ b/solution.py
@@ -420,7 +420,8 @@
     for k in spread_out:
         send_part(k).start()
     start_all(send_b, 1)
-    start_all(send_b, 2)
+    for k in pan_batches[2][::-1]:
+        send_b(k).start()
 
     def forward_y(j):
         device = (rep, y * side + lax.rem(z + 1 + j, side))

time: 67.4 us -> 67.5 us (level)
  no operation moved by 1% of the time
where the time goes in v6:
time: 67.5 us; the launch traced here: 67.1 us
  Pallas kernels  65.4 us (97%)
  local copies, waits for them, and re-layouts  1.67 us (2%)
    pallas_call x1, Pallas kernels, shards(): pl.pallas_call(functools.partial(kernel, n_rep, n_tp, side), out_shape=ja...  65.4 us
    unnamed x1, local copies, waits for them, and re-layouts  1.67 us

profile of v6, /device:TPU:0, one launch (start us, length us, event | category | flops | bytes accessed | tf_op | source)
XLA Modules:
  0.0 67.1 jit_solution(403051504631053854)
XLA Ops:
  0.0 65.4 %shard_map.82 = bf16[4,64,512]{2,1,0:T(8,128)(2,1)} custom-call(bf16[4,64,512]{2,1,0:T(8,128)(2,1)} %queries.1, bf16[4,64,2048]{2,1,0:T(8,128)(2,1)} %new_kv.1, bf16[32,512,256]{2,1,0:T(8,128)(2,1)} %kv_cache.1, s32[4,64]{1,0:T(4,128)} %lengths.1, s32[4,64]{1,0:T(4,128)} %ids.1, s32[1,128]{1,0:T(1,128)} %bitcast.1, bf16[1,8192,128]{2,1,0:T(8,128)(2,1)} %panels.1, ...), custom_call_target="tpu_custom_call" | custom-call | flops 5000000000 | bytes 20000000 | tf_op jit(solution)/shard_map/pallas_call | solution.py:600
  65.4 1.7 %copy.10 = bf16[4,64,512]{2,1,0:T(8,128)(2,1)} copy(bf16[4,64,512]{2,1,0:T(8,128)(2,1)} %shard_map.82) | data formatting | bytes 524288
